TPU v7x, 256 devices: a whole 4x4x8 slice. The times are simulated.
256 devices in a mesh: dp: 32 (over z, y_lo, core), replica: 8 (over x, y_hi).
Axes of the slice: x: 4, y: 4 (y_hi: 2, y_lo: 2; y = y_hi * 2 + y_lo), z: 8, core: 2. Of those that a mesh axis runs over, the one named last changes fastest.
Arguments:
- picture_encoder_features: bfloat16 [57344, 1152], P(('dp', 'replica')), may hold values from -24 to 24
- text_encoder_features: bfloat16 [57344, 1152], P(('dp', 'replica')), may hold values from -24 to 24
- picture_projector: bfloat16 [1152, 1152], replicated, may hold values from -0.1875 to 0.1875
- text_projector: bfloat16 [1152, 1152], replicated, may hold values from -0.1875 to 0.1875
- matching_target: int32 [57344], P(('dp', 'replica')), may hold values from 0 to 223, as said below
- sharpness_param: float32 [1], replicated, may hold values from 10 to 40
- offset_shift: float32 [1], replicated, may hold values from -4 to -1
- objective_multiplier: float32 [1], replicated, may hold values from 64 to 512
Outputs:
- grad_image_head: float32 [1152, 1152], P('dp')
- grad_caption_head: float32 [1152, 1152], P('dp')
Inputs may be any that keep to these rules, and one draw needn't show every extreme that they name: Within each device's 224 rows the entries are a permutation of 0 to 223: image row r of a block matches caption row matching_target[r] of the same block.
All inputs are finite; a program needn't handle non-finite values.
Results may differ from a plain program's by a relative error of at most 0.0025.
Values may be sent and summed in bfloat16 or wider, within the bound.
No kernel may reach another device: no remote copies, remote signals or barrier semaphores. Data moves between devices by JAX's collectives and lax.ppermute only.
A program may use at most 128 MiB of HBM per device.

v0:
```python
import jax
import jax.numpy as jnp
import numpy as np
from jax import lax
from jax.experimental import pallas as pl
from jax.experimental.pallas import tpu as pltpu
from jax.sharding import PartitionSpec as P

AXES = ("dp", "replica")
NX, NY, NZ = 4, 4, 8
R, D, PAD = 224, 1152, 256
F32, BF16 = jnp.float32, jnp.bfloat16


def device_at(x, y, z, core):
    x, y, z = x % NX, y % NY, z % NZ
    return (z * 4 + (y % 2) * 2 + core) * 8 + x * 2 + y // 2


PLACES = [(x, y, z, c) for x in range(NX) for y in range(NY) for z in range(NZ) for c in range(2)]


ALONG_Z = [[device_at(x, y, z, c) for z in range(NZ)] for x in range(NX) for y in range(NY) for c in range(2)]


def row_order(core, x, y):
    rows = np.arange(D)
    ninth, z = rows % 9, rows // 9 % 8
    one, two = rows // 288, rows // 72 % 4
    to_x = (x + jnp.where(core == 0, one, two)) % NX
    to_y = (y + jnp.where(core == 0, two, one)) % NY
    return (z * 2 + to_y % 2) * 72 + to_y // 2 * 36 + to_x * 9 + ninth


def moved(value, to):
    pairs = []
    for place in PLACES:
        target = to(*place)
        if target is not None:
            pairs.append((device_at(*place), device_at(*target)))
    return lax.ppermute(value, AXES, pairs)


def swap_cores(value):
    return moved(value, lambda x, y, z, c: (x, y, z, 1 - c))


def swap_chips(value):
    return moved(value, lambda x, y, z, c: (x, y ^ 1, z, c))


def image_to_neighbour(value):
    return moved(value, lambda x, y, z, c: (x, y, z - 1, c) if y % 2 == 0 else (x, y, z + 1, c))


def first_axis(value, by):
    return moved(value, lambda x, y, z, c: (x + by, y, z, c) if c == 0 else (x, y + by, z, c))


def second_axis(value, by):
    return moved(value, lambda x, y, z, c: (x, y + by, z, c) if c == 0 else (x + by, y, z, c))


def along_x(value, by):
    return moved(value, lambda x, y, z, c: (x + by, y, z, c))


def pass_on(value):
    def to(x, y, z, c):
        if c == y // 2:
            return (x, y ^ 2, z, c)
        return (x, y, z, 1 - c)

    return moved(value, to)


def pass_across(value):
    return moved(value, lambda x, y, z, c: (x, y ^ 2, z, 1 - c) if c != y // 2 else None)


def image_down(value):
    return moved(value, lambda x, y, z, c: (x, y, z - 1, c) if y % 2 == 1 and c == 0 else None)


THIRDS = [(n, 384) for n in range(0, D, 384)]


def nt_dot(a, b):
    return lax.dot_general(a, b, (((1,), (1,)), ((), ())), preferred_element_type=F32)


def fetch(src, dst, sem):
    copy = pltpu.make_async_copy(src, dst, sem)
    copy.start()
    return copy


def by_role(core_ref, choices, sems):
    waits = []
    for k, (zero, one, dst) in enumerate(choices):

        @pl.when(core_ref[0] == 0)
        def _():
            fetch(zero, dst, sems.at[k])

        @pl.when(core_ref[0] == 1)
        def _():
            fetch(one, dst, sems.at[k])

        waits.append(pltpu.make_async_copy(zero, dst, sems.at[k]))
    return waits


def project(feats, head, tmp, rows):
    squares = jnp.zeros((rows, 1), F32)
    for n, w in THIRDS:
        p = jnp.dot(feats, head[:, n : n + w], preferred_element_type=F32)
        tmp[0:rows, n : n + w] = p
        squares = squares + jnp.sum(p * p, axis=1, keepdims=True)
    return lax.rsqrt(squares + 1e-6)


def pair_weights(scal_ref, rows, cols, xs, height, ys, gs, signs=None):
    logits = nt_dot(rows, cols) * scal_ref[0] + scal_ref[1]
    for i, x in enumerate(xs):
        for j, y in enumerate(ys):
            part = logits[i * height : (i + 1) * height, j * PAD : (j + 1) * PAD]
            scale = scal_ref[2 + x * 5 + y]
            if signs is not None and x == y:
                sign = signs[x]
                g = (scale * sign) * jax.nn.sigmoid(sign * part)
            else:
                g = scale * jax.nn.sigmoid(part)
            gs[i * height : (i + 1) * height, j * PAD : (j + 1) * PAD] = g.astype(BF16)


def own_kernel(
    core_ref, scal_ref, lab_ref, im, io, cm, co, wi, wc, order,
    zx, zy, ux, ix, ft, dz,
    f, w, pv, lab, tmp, gs, sems,
):
    waits = by_role(
        core_ref,
        [
            (im, co, f.at[0, pl.ds(0, R)]), (io, cm, f.at[0, pl.ds(R, R)]),
            (cm, io, f.at[1, pl.ds(0, R)]), (co, im, f.at[1, pl.ds(R, R)]),
            (wi, wc, w.at[0]), (wc, wi, w.at[1]),
        ],
        sems,
    )
    late = [fetch(order, pv, sems.at[6]), fetch(lab_ref, lab, sems.at[7])]
    for wait in waits:
        wait.wait()
    inv = project(f[0], w.at[0], tmp, 2 * R)
    ix[...] = jnp.broadcast_to(inv, (2 * R, 128))
    for n, wd in THIRDS:
        unit = tmp[:, n : n + wd] * inv
        ux[:, n : n + wd] = unit
        zx[:, n : n + wd] = unit.astype(BF16)
    inv = project(f[1], w.at[1], tmp, 2 * R)
    for b in range(2):
        zy[b * PAD : b * PAD + R] = (tmp[b * R : (b + 1) * R] * inv[b * R : (b + 1) * R]).astype(BF16)
        zy[b * PAD + R : (b + 1) * PAD] = jnp.zeros((PAD - R, D), BF16)
    for copy in late:
        copy.wait()

    @pl.loop(0, 3)
    def _(k):
        rows = pl.ds(pl.multiple_of(k * 384, 384), 384)
        ft[rows, 0 : 2 * R] = nt_dot(pv[rows], f[0]).astype(BF16)

    ft[:, 2 * R :] = jnp.zeros((D, 2 * PAD - 2 * R), BF16)
    pair_weights(scal_ref, zx[...], zy[...], (0, 1), R, (0, 1), gs, lab)

    @pl.loop(0, 3)
    def _(k):
        cols = pl.ds(pl.multiple_of(k * 384, 384), 384)
        dz[:, cols] = scal_ref[0] * jnp.dot(gs[...], zy[:, cols], preferred_element_type=F32)


def own_part(core, scal, lab, im, io, cm, co, wi, wc, order):
    smem = pl.BlockSpec(memory_space=pltpu.SMEM)
    vmem = pl.BlockSpec(memory_space=pltpu.VMEM)
    return pl.pallas_call(
        own_kernel,
        out_shape=[
            jax.ShapeDtypeStruct((2 * R, D), BF16),
            jax.ShapeDtypeStruct((2 * PAD, D), BF16),
            jax.ShapeDtypeStruct((2 * R, D), F32),
            jax.ShapeDtypeStruct((2 * R, 128), F32),
            jax.ShapeDtypeStruct((D, 2 * PAD), BF16),
            jax.ShapeDtypeStruct((2 * R, D), F32),
        ],
        in_specs=[smem, smem] + [pl.BlockSpec(memory_space=pl.ANY)] * 8,
        out_specs=[vmem] * 6,
        scratch_shapes=[
            pltpu.VMEM((2, 2 * R, D), BF16),
            pltpu.VMEM((2, D, D), BF16),
            pltpu.VMEM((D, D), BF16),
            pltpu.VMEM((2, R, PAD), F32),
            pltpu.VMEM((2 * R, D), F32),
            pltpu.VMEM((2 * R, 2 * PAD), BF16),
            pltpu.SemaphoreType.DMA((8,)),
        ],
        compiler_params=pltpu.CompilerParams(vmem_limit_bytes=60 * 2**20),
        cost_estimate=pl.CostEstimate(flops=6 * 10**9, bytes_accessed=16 * 10**6, transcendentals=230000),
    )(core, scal, lab, im, io, cm, co, wi, wc, order)


def arrived_kernel(
    core_ref, scal_ref, sm, so, fm, fo, em, eo, wi, wc, order, zx_in, zy_in, ux_in, ix_in, ft_in, dz_in,
    out0, out1, out2, out3,
    f, w, pv, zx, z, uo, ua, io_, ia, fto, fta, dz, da, gs, dp, tmp, sems,
):
    role = core_ref[0]
    gap = PAD - R
    rows_first = by_role(
        core_ref,
        [(fm, so, f.at[0, pl.ds(0, R)]), (fo, sm, f.at[1, pl.ds(0, R)]), (wi, wc, w.at[0])],
        sems.at[pl.ds(0, 3)],
    )
    cols_next = by_role(
        core_ref,
        [(sm, fo, f.at[3, pl.ds(0, R)]), (so, fm, f.at[4, pl.ds(0, R)]), (wc, wi, w.at[1])],
        sems.at[pl.ds(3, 3)],
    )

    @pl.when(role == 0)
    def _():
        fetch(em, f.at[2, pl.ds(0, R)], sems.at[6])
        f[5] = jnp.zeros((PAD, D), BF16)
        z[7 * PAD : 8 * PAD] = jnp.zeros((PAD, D), BF16)

    @pl.when(role == 1)
    def _():
        fetch(eo, f.at[5, pl.ds(0, R)], sems.at[6])
        f[2] = jnp.zeros((PAD, D), BF16)
        z[2 * PAD : 3 * PAD] = jnp.zeros((PAD, D), BF16)
        ua[2 * PAD : 3 * PAD] = jnp.zeros((PAD, D), F32)
        ia[2 * PAD : 3 * PAD] = jnp.zeros((PAD, 128), F32)

    for s in range(3):
        f[s, R:PAD] = jnp.zeros((gap, D), BF16)
        ua[s * PAD + R : (s + 1) * PAD] = jnp.zeros((gap, D), F32)
        ia[s * PAD + R : (s + 1) * PAD] = jnp.zeros((gap, 128), F32)
        z[s * PAD + R : (s + 1) * PAD] = jnp.zeros((gap, D), BF16)
        z[(s + 5) * PAD + R : (s + 6) * PAD] = jnp.zeros((gap, D), BF16)
    dp[2 * R : 2 * PAD] = jnp.zeros((2 * gap, D), BF16)
    extra = pltpu.make_async_copy(em, f.at[2, pl.ds(0, R)], sems.at[6])
    for wait in rows_first + [extra]:
        wait.wait()
    late = [
        fetch(order, pv, sems.at[7]),
        fetch(zx_in, zx, sems.at[8]),
        fetch(zy_in, z.at[pl.ds(3 * PAD, 2 * PAD)], sems.at[9]),
        fetch(ux_in, uo, sems.at[10]),
        fetch(ix_in, io_, sems.at[11]),
        fetch(dz_in, dz, sems.at[12]),
        fetch(ft_in, fto, sems.at[13]),
    ]

    @pl.loop(0, 3 - role)
    def _(k):
        inv = project(f[k, 0:R], w.at[0], tmp, R)
        rows = pl.ds(pl.multiple_of(k * PAD, PAD), R)
        unit = tmp[...] * inv
        z[rows] = unit.astype(BF16)
        ua[rows] = unit
        ia[rows] = jnp.broadcast_to(inv, (R, 128))

    for wait in cols_next:
        wait.wait()

    @pl.loop(0, 2 + role)
    def _(k):
        inv = project(f[k + 3, 0:R], w.at[1], tmp, R)
        z[pl.ds(pl.multiple_of((k + 5) * PAD, PAD), R)] = (tmp[...] * inv).astype(BF16)

    for copy in late:
        copy.wait()

    @pl.loop(0, 3)
    def _(k):
        rows = pl.ds(pl.multiple_of(k * 384, 384), 384)
        fta[rows] = nt_dot(pv[rows], f[0:3].reshape(3 * PAD, D)).astype(BF16)

    def spread(m, cols, y0, y1, kept, unit, inverse, base):
        @pl.loop(0, 3)
        def _(k):
            at = pl.ds(pl.multiple_of(k * 384, 384), 384)
            d = scal_ref[0] * jnp.dot(gs[0:m, 0:cols], z[y0 * PAD : y1 * PAD, at], preferred_element_type=F32)
            if kept:
                d = d + dz[:, at]
            da[0:m, at] = d

        along = jnp.sum(da[0:m] * unit[0:m], axis=1, keepdims=True)
        dp[base : base + m] = ((da[0:m] - unit[0:m] * along) * inverse[0:m, 0:1]).astype(BF16)

    @pl.when(role == 0)
    def _():
        pair_weights(scal_ref, zx[...], z[5 * PAD : 7 * PAD], (0, 1), R, (2, 3), gs)
        spread(2 * R, 2 * PAD, 5, 7, True, uo, io_, 0)
        pair_weights(scal_ref, z[0 : 2 * PAD], z[4 * PAD : 7 * PAD], (2, 3), PAD, (1, 2, 3), gs)
        spread(2 * PAD, 3 * PAD, 4, 7, False, ua, ia, 2 * PAD)
        pair_weights(scal_ref, z[2 * PAD : 3 * PAD], z[4 * PAD : 5 * PAD], (4,), PAD, (1,), gs)
        spread(PAD, PAD, 4, 5, False, ua.at[2 * PAD : 3 * PAD], ia.at[2 * PAD : 3 * PAD], 4 * PAD)

    @pl.when(role == 1)
    def _():
        pair_weights(scal_ref, zx[...], z[5 * PAD : 8 * PAD], (0, 1), R, (2, 3, 4), gs)
        spread(2 * R, 3 * PAD, 5, 8, True, uo, io_, 0)
        pair_weights(scal_ref, z[0 : 2 * PAD], z[3 * PAD : 7 * PAD], (2, 3), PAD, (0, 1, 2, 3), gs)
        spread(2 * PAD, 4 * PAD, 3, 7, False, ua, ia, 2 * PAD)
        dp[4 * PAD : 5 * PAD] = jnp.zeros((PAD, D), BF16)

    @pl.loop(0, 3)
    def _(k):
        at = pl.ds(pl.multiple_of(k * 384, 384), 384)
        own = dp[0 : 2 * PAD, at]
        rest = dp[2 * PAD : 5 * PAD, at]
        for i, out in enumerate((out0, out1, out2, out3)):
            rows = slice(i * 288, (i + 1) * 288)
            out[:, at] = (
                jnp.dot(fto[rows], own, preferred_element_type=F32)
                + jnp.dot(fta[rows], rest, preferred_element_type=F32)
            ).astype(BF16)


def arrived_part(core, scal, *operands):
    smem = pl.BlockSpec(memory_space=pltpu.SMEM)
    vmem = pl.BlockSpec(memory_space=pltpu.VMEM)
    return pl.pallas_call(
        arrived_kernel,
        out_shape=[jax.ShapeDtypeStruct((D // 4, D), BF16)] * 4,
        in_specs=[smem, smem] + [pl.BlockSpec(memory_space=pl.ANY)] * 15,
        out_specs=[vmem] * 4,
        scratch_shapes=[
            pltpu.VMEM((6, PAD, D), BF16),
            pltpu.VMEM((2, D, D), BF16),
            pltpu.VMEM((D, D), BF16),
            pltpu.VMEM((2 * R, D), BF16),
            pltpu.VMEM((8 * PAD, D), BF16),
            pltpu.VMEM((2 * R, D), F32),
            pltpu.VMEM((3 * PAD, D), F32),
            pltpu.VMEM((2 * R, 128), F32),
            pltpu.VMEM((3 * PAD, 128), F32),
            pltpu.VMEM((D, 2 * PAD), BF16),
            pltpu.VMEM((D, 3 * PAD), BF16),
            pltpu.VMEM((2 * R, D), F32),
            pltpu.VMEM((3 * PAD, D), F32),
            pltpu.VMEM((3 * PAD, 4 * PAD), BF16),
            pltpu.VMEM((5 * PAD, D), BF16),
            pltpu.VMEM((R, D), F32),
            pltpu.SemaphoreType.DMA((14,)),
        ],
        compiler_params=pltpu.CompilerParams(vmem_limit_bytes=60 * 2**20),
        cost_estimate=pl.CostEstimate(flops=14 * 10**9, bytes_accessed=20 * 10**6, transcendentals=800000),
    )(core, scal, *operands)


def local(
    picture_encoder_features,
    text_encoder_features,
    picture_projector,
    text_projector,
    matching_target,
    sharpness_param,
    offset_shift,
    objective_multiplier,
):
    place = lax.axis_index("dp")
    core, y_lo = place % 2, (place // 2) % 2
    x, y_hi = lax.axis_index("replica") // 2, lax.axis_index("replica") % 2
    y = y_hi * 2 + y_lo
    coefficient = objective_multiplier[0] / (lax.axis_size("dp") * R)

    cap_sib = swap_chips(text_encoder_features)
    img_far = image_to_neighbour(picture_encoder_features)
    img_extra = image_down(picture_encoder_features)
    target_other = swap_cores(matching_target)
    cap_sib_other = swap_cores(cap_sib)
    img_far_other = swap_cores(img_far)
    img_extra_other = swap_cores(img_extra)

    even = y_lo == 0
    img_at = np.array([[0, 1, 4, 5, 100], [2, 3, -2, -1, 6]])
    cap_at = np.array([[0, 1, 2, 3], [2, 3, 0, 1]])
    apart = cap_at[:, None, :] - img_at[:, :, None]
    taken = np.pad(((apart >= -3) & (apart <= 2)).astype(np.float32), ((0, 0), (0, 0), (0, 1)))
    first = core == 0
    taken = jnp.where(even, taken[0], taken[1])
    scales = coefficient * jnp.where(first, taken, taken.T)
    scalars = jnp.concatenate([sharpness_param, offset_shift, scales.reshape(-1)])
    targets = jnp.stack(
        [jnp.where(first, matching_target, target_other), jnp.where(first, target_other, matching_target)]
    )
    column = lax.broadcasted_iota(jnp.int32, (2, R, PAD), 2)
    row = lax.broadcasted_iota(jnp.int32, (2, R, PAD), 1)
    wide = jnp.pad(targets, ((0, 0), (0, PAD - R)), constant_values=-1)
    match = jnp.where(first, column == targets[:, :, None], row == wide[:, None, :])
    signs = jnp.where(match, -1.0, 1.0).astype(F32)
    order = row_order(core, x, y).astype(jnp.int32)
    one_hot = (lax.broadcasted_iota(jnp.int32, (D, D), 1) == order[:, None]).astype(BF16)

    role = core[None].astype(jnp.int32)
    img, cap, one_hot = lax.optimization_barrier(
        (picture_encoder_features, text_encoder_features, one_hot)
    )
    own_img = swap_cores(img)
    own_cap = swap_cores(cap)
    kept = own_part(
        role, scalars, signs, picture_encoder_features, own_img, text_encoder_features, own_cap,
        picture_projector, text_projector, one_hot,
    )
    parts = arrived_part(
        role, scalars, cap_sib, cap_sib_other, img_far, img_far_other, img_extra, img_extra_other,
        picture_projector, text_projector, one_hot, *kept,
    )

    one = [parts[0]] + [first_axis(parts[by], by) for by in (1, 3, 2)]
    one = sum(v.astype(F32) for v in one).astype(BF16)
    pieces = [one[by * 72 : (by + 1) * 72] for by in range(4)]
    two = [pieces[0]] + [second_axis(pieces[by], by) for by in (1, 3, 2)]
    two = sum(v.astype(F32) for v in two).astype(BF16).reshape(NZ, 81, 128)
    three = lax.all_to_all(two, AXES, 0, 0, axis_index_groups=ALONG_Z)
    mine = jnp.sum(three.astype(F32), axis=0)

    ring, cross = pass_on(mine), pass_across(mine)
    home = core == y_hi
    image_piece = jnp.where(home & first, mine, jnp.where(home | first, ring, cross))
    caption_piece = jnp.where(home & first, ring, jnp.where(home, mine, jnp.where(first, cross, ring)))
    both = jnp.stack([image_piece, caption_piece])
    held = jnp.stack([both] + [along_x(both, by) for by in (1, 2, 3)])
    rows = jnp.take(held, (x - jnp.arange(NX)) % NX, axis=0).transpose(1, 0, 2, 3).reshape(2, 36, D)
    return (rows[0], rows[1])


def solution(mesh):
    placed = (
        P(("dp", "replica"), None),
        P(("dp", "replica"), None),
        P(),
        P(),
        P(("dp", "replica")),
        P(),
        P(),
        P(),
    )
    return jax.shard_map(
        local, mesh=mesh, in_specs=placed, out_specs=(P("dp", None), P("dp", None)), check_vma=False
    )
```

profile of v0, /device:TPU:1, one launch (start us, length us, event | category | flops | bytes accessed | tf_op | source)
XLA Modules:
  0.0 130.1 jit_solution(5576078200469893806)
XLA Ops:
  0.6 6.5 %collective-permute-start.2 = (bf16[224,1152]{1,0:T(8,128)(2,1)}, bf16[224,1152]{1,0:T(8,128)(2,1)S(1)}, u32[]{:S(2)}, u32[]{:S(2)}) collective-permute-start(bf16[224,1152]{1,0:T(8,128)(2,1)} %im.1), channel_id=1, source_target_pairs={{0,224},{8,232},{32,0},{40,8},{64,32},{72,40},{96,64},{104,72},{12... | collective-permute-start | bytes 1548296 | tf_op jit(solution)/shard_map/ppermute | solution.py:41
  8.0 0.8 fusion.8
  8.8 2.0 %fusion.order = bf16[1152,1152]{1,0:T(8,128)(2,1)} fusion(s32[1152]{0:T(1024)S(1)} %fusion.8), kind=kLoop, calls=%fused_computation.2 | loop fusion | flops 2654208 | bytes 2658816 | tf_op jit(solution)/shard_map/convert_element_type | solution.py:403
  10.8 3.7 %collective-permute-start.7 = (bf16[224,1152]{1,0:T(8,128)(2,1)S(1)}, bf16[224,1152]{1,0:T(8,128)(2,1)S(1)}, u32[]{:S(2)}, u32[]{:S(2)}) collective-permute-start(bf16[224,1152]{1,0:T(8,128)(2,1)S(1)} %copy-done.4), channel_id=1, source_target_pairs={{0,8},{8,0},{32,40},{40,32},{64,72},{72,64},{96,104},{104,96},{128... | collective-permute-start | bytes 1548296 | tf_op jit(solution)/shard_map/ppermute | solution.py:41
  17.8 0.9 fusion.2.lab_ref
  18.7 0.9 collective-permute-done.sm
  19.6 2.7 %collective-permute-start.1 = (bf16[224,1152]{1,0:T(8,128)(2,1)S(1)}, bf16[224,1152]{1,0:T(8,128)(2,1)S(1)}, u32[]{:S(2)}, u32[]{:S(2)}) collective-permute-start(bf16[224,1152]{1,0:T(8,128)(2,1)S(1)} %collective-permute-done.sm), channel_id=1, source_target_pairs={{0,8},{8,0},{32,40},{40,32},{64,72},{72,64},{96,104},{104,96},{128... | collective-permute-start | bytes 1548296 | tf_op jit(solution)/shard_map/ppermute | solution.py:41
  22.8 0.8 copy-done.10
  23.8 14.6 %shard_map.149 = (bf16[448,1152]{1,0:T(8,128)(2,1)}, bf16[512,1152]{1,0:T(8,128)(2,1)}, f32[448,1152]{1,0:T(8,128)}, f32[448,128]{1,0:T(8,128)}, bf16[1152,512]{1,0:T(8,128)(2,1)}, /*index=5*/f32[448,1152]{1,0:T(8,128)}) custom-call(s32[1]{0:T(128)} %bitcast.core_ref, f32[27]{0:T(128)} %pad_maximum_fusion.2.scal_ref, f32[2,224,256]{2,1,0:T(8,128)} %fusion.2.lab_ref, ...), custom_call_target="tpu_custom_call" | custom-call | flops 6000000000 | bytes 16000000 | tf_op jit(solution)/shard_map/pallas_call | solution.py:184
  39.2 26.1 %shard_map.150 = (bf16[288,1152]{1,0:T(8,128)(2,1)}, bf16[288,1152]{1,0:T(8,128)(2,1)}, bf16[288,1152]{1,0:T(8,128)(2,1)}, bf16[288,1152]{1,0:T(8,128)(2,1)}) custom-call(s32[1]{0:T(128)} %bitcast.core_ref, f32[27]{0:T(128)} %pad_maximum_fusion.2.scal_ref, bf16[224,1152]{1,0:T(8,128)(2,1)} %copy-done.7, bf16[224,1152]{1,0:T(8,128)(2,1)} %copy-done.9, ...), custom_call_target="tpu_custom_call" | custom-call | flops 14000000000 | bytes 20000000 | tf_op jit(solution)/shard_map/pallas_call | solution.py:332
  65.3 1.8 %collective-permute-start.10 = (bf16[288,1152]{1,0:T(8,128)(2,1)}, bf16[288,1152]{1,0:T(8,128)(2,1)S(1)}, u32[]{:S(2)}, u32[]{:S(2)}) collective-permute-start(bf16[288,1152]{1,0:T(8,128)(2,1)} %get-tuple-element.26), channel_id=1, source_target_pairs={{0,6},{8,25},{32,38},{40,57},{64,70},{72,89},{96,102},{104,121},{1... | collective-permute-start | bytes 1990664 | tf_op jit(solution)/shard_map/ppermute | solution.py:41
  67.1 1.3 collective-permute-start.11
  69.2 13.0 %collective-permute-done.10 = bf16[288,1152]{1,0:T(8,128)(2,1)S(1)} collective-permute-done((bf16[288,1152]{1,0:T(8,128)(2,1)}, bf16[288,1152]{1,0:T(8,128)(2,1)S(1)}, u32[]{:S(2)}, u32[]{:S(2)}) %collective-permute-start.10) | collective-permute-done | bytes 663584 | tf_op jit(solution)/shard_map/ppermute | solution.py:41
  82.2 3.6 %collective-permute-done.9 = bf16[288,1152]{1,0:T(8,128)(2,1)S(1)} collective-permute-done((bf16[288,1152]{1,0:T(8,128)(2,1)}, bf16[288,1152]{1,0:T(8,128)(2,1)S(1)}, u32[]{:S(2)}, u32[]{:S(2)}) %collective-permute-start.9) | collective-permute-done | bytes 663584 | tf_op jit(solution)/shard_map/ppermute | solution.py:41
  85.8 1.4 %add_convert_fusion = bf16[288,1152]{1,0:T(8,128)(2,1)S(1)} fusion(bf16[288,1152]{1,0:T(8,128)(2,1)S(1)} %collective-permute-done.11, bf16[288,1152]{1,0:T(8,128)(2,1)S(1)} %collective-permute-done.10, bf16[288,1152]{1,0:T(8,128)(2,1)S(1)} %collective-permute-done.9, bf16[288,1152]{1,0:T(8,128)(2,1)} %get-tuple-element.24), kind=kLoop, calls=%fused_computation.3 | loop fusion | flops 2654208 | bytes 3317760 | tf_op jit(solution)/shard_map/convert_element_type | solution.py:421
  87.3 1.0 collective-permute-start.12
  88.3 1.8 %collective-permute-start.13 = (bf16[72,1152]{1,0:T(8,128)(2,1)S(1)}, bf16[72,1152]{1,0:T(8,128)(2,1)S(1)}, u32[]{:S(2)}, u32[]{:S(2)}) collective-permute-start(bf16[72,1152]{1,0:T(8,128)(2,1)S(1)} %get-tuple-element.32), channel_id=1, source_target_pairs={{0,17},{8,14},{32,49},{40,46},{64,81},{72,78},{96,113},{104,110},{... | collective-permute-start | bytes 497672 | tf_op jit(solution)/shard_map/ppermute | solution.py:41
  90.0 1.2 collective-permute-start.14
  91.3 1.5 %collective-permute-done.12 = bf16[72,1152]{1,0:T(8,128)(2,1)S(1)} collective-permute-done((bf16[72,1152]{1,0:T(8,128)(2,1)S(1)}, bf16[72,1152]{1,0:T(8,128)(2,1)S(1)}, u32[]{:S(2)}, u32[]{:S(2)}) %collective-permute-start.12) | collective-permute-done | bytes 165920 | tf_op jit(solution)/shard_map/ppermute | solution.py:41
  92.7 1.3 %collective-permute-done.13 = bf16[72,1152]{1,0:T(8,128)(2,1)S(1)} collective-permute-done((bf16[72,1152]{1,0:T(8,128)(2,1)S(1)}, bf16[72,1152]{1,0:T(8,128)(2,1)S(1)}, u32[]{:S(2)}, u32[]{:S(2)}) %collective-permute-start.13) | collective-permute-done | bytes 165920 | tf_op jit(solution)/shard_map/ppermute | solution.py:41
  94.1 1.6 %collective-permute-done.14 = bf16[72,1152]{1,0:T(8,128)(2,1)S(1)} collective-permute-done((bf16[72,1152]{1,0:T(8,128)(2,1)S(1)}, bf16[72,1152]{1,0:T(8,128)(2,1)S(1)}, u32[]{:S(2)}, u32[]{:S(2)}) %collective-permute-start.14) | collective-permute-done | bytes 165920 | tf_op jit(solution)/shard_map/ppermute | solution.py:41
  95.8 0.9 reshape.75
  96.7 4.6 %all-to-all-start = ((bf16[8,81,128]{2,1,0:T(8,128)(2,1)}), bf16[8,81,128]{2,1,0:T(8,128)(2,1)S(1)}, u32[]{:S(2)}, u32[]{:S(2)}) async-start(bf16[8,81,128]{2,1,0:T(8,128)(2,1)} %reshape.75), calls=%async_computation | async-start | bytes 360448 | tf_op jit(solution)/shard_map/all_to_all | solution.py:425
  101.3 8.5 %all-to-all-done = bf16[8,81,128]{2,1,0:T(8,128)(2,1)S(1)} async-done(((bf16[8,81,128]{2,1,0:T(8,128)(2,1)}), bf16[8,81,128]{2,1,0:T(8,128)(2,1)S(1)}, u32[]{:S(2)}, u32[]{:S(2)}) %all-to-all-start) | async-done | bytes 165920 | tf_op jit(solution)/shard_map/all_to_all | solution.py:425
  109.9 3.5 %collective-permute-start.15 = (f32[81,128]{1,0:T(8,128)S(1)}, f32[81,128]{1,0:T(8,128)S(1)}, u32[]{:S(2)}, u32[]{:S(2)}) collective-permute-start(f32[81,128]{1,0:T(8,128)S(1)} %convert_reduce_fusion), channel_id=1, source_target_pairs={{0,1},{8,0},{32,33},{40,32},{64,65},{72,64},{96,97},{104,96},{128,... | collective-permute-start | bytes 124424 | tf_op jit(solution)/shard_map/ppermute | solution.py:41
  113.4 3.3 %collective-permute-start.16 = (f32[81,128]{1,0:T(8,128)S(1)}, f32[81,128]{1,0:T(8,128)S(1)}, u32[]{:S(2)}, u32[]{:S(2)}) collective-permute-start(f32[81,128]{1,0:T(8,128)S(1)} %convert_reduce_fusion), channel_id=1, source_target_pairs={{8,1},{40,33},{72,65},{104,97},{136,129},{168,161},{200,193},{232,... | collective-permute-start | bytes 124424 | tf_op jit(solution)/shard_map/ppermute | solution.py:41
  116.8 3.5 %collective-permute-done.16 = f32[81,128]{1,0:T(8,128)S(1)} collective-permute-done((f32[81,128]{1,0:T(8,128)S(1)}, f32[81,128]{1,0:T(8,128)S(1)}, u32[]{:S(2)}, u32[]{:S(2)}) %collective-permute-start.16) | collective-permute-done | bytes 41504 | tf_op jit(solution)/shard_map/ppermute | solution.py:41
  120.6 1.8 %collective-permute-start.18 = (f32[2,81,128]{2,0,1:T(2,128)S(1)}, f32[2,81,128]{2,0,1:T(2,128)S(1)}, u32[]{:S(2)}, u32[]{:S(2)}) collective-permute-start(f32[2,81,128]{2,0,1:T(2,128)S(1)} %get-tuple-element.36), channel_id=1, source_target_pairs={{0,4},{8,12},{32,36},{40,44},{64,68},{72,76},{96,100},{104,108},{1... | collective-permute-start | bytes 248840 | tf_op jit(solution)/shard_map/ppermute | solution.py:41
  122.3 0.9 collective-permute-start.19
  123.3 2.7 %collective-permute-done.17 = f32[2,81,128]{2,0,1:T(2,128)S(1)} collective-permute-done((f32[2,81,128]{2,0,1:T(2,128)S(1)}, f32[2,81,128]{2,0,1:T(2,128)S(1)}, u32[]{:S(2)}, u32[]{:S(2)}) %collective-permute-start.17) | collective-permute-done | bytes 82976 | tf_op jit(solution)/shard_map/ppermute | solution.py:41
  126.7 0.9 gather_fusion
  127.8 0.9 slice_reduce_fusion
  (63 shorter events, 7.1 us)
Async XLA Ops:
  0.6 21.6 %collective-permute-start.2 = (bf16[224,1152]{1,0:T(8,128)(2,1)}, bf16[224,1152]{1,0:T(8,128)(2,1)S(1)}, u32[]{:S(2)}, u32[]{:S(2)}) collective-permute-start(bf16[224,1152]{1,0:T(8,128)(2,1)} %im.1), channel_id=1, source_target_pairs={{0,224},{8,232},{32,0},{40,8},{64,32},{72,40},{96,64},{104,72},{12... | collective-permute-start | bytes 1548296 | tf_op jit(solution)/shard_map/ppermute | solution.py:41
  7.1 15.3 %collective-permute-start.4 = (bf16[224,1152]{1,0:T(8,128)(2,1)}, bf16[224,1152]{1,0:T(8,128)(2,1)S(1)}, u32[]{:S(2)}, u32[]{:S(2)}) collective-permute-start(bf16[224,1152]{1,0:T(8,128)(2,1)} %im.1), channel_id=1, source_target_pairs={{16,240},{48,16},{80,48},{112,80},{144,112},{176,144},{208,176},{2... | collective-permute-start | bytes 1548296 | tf_op jit(solution)/shard_map/ppermute | solution.py:41
  7.8 11.8 %collective-permute-start = (bf16[224,1152]{1,0:T(8,128)(2,1)}, bf16[224,1152]{1,0:T(8,128)(2,1)S(1)}, u32[]{:S(2)}, u32[]{:S(2)}) collective-permute-start(bf16[224,1152]{1,0:T(8,128)(2,1)} %cm.1), channel_id=1, source_target_pairs={{0,16},{8,24},{32,48},{40,56},{64,80},{72,88},{96,112},{104,120},{... | collective-permute-start | bytes 1548296 | tf_op jit(solution)/shard_map/ppermute | solution.py:41
  8.7 2.1 %copy-start.4 = (bf16[224,1152]{1,0:T(8,128)(2,1)S(1)}, bf16[224,1152]{1,0:T(8,128)(2,1)}, u32[]{:S(2)}) copy-start(bf16[224,1152]{1,0:T(8,128)(2,1)} %im.1) | copy-start | bytes 1548292
  8.7 5.8 %copy-start.2 = (s32[224]{0:T(256)S(1)}, s32[224]{0:T(256)}, u32[]{:S(2)}) copy-start(s32[224]{0:T(256)} %param.18) | copy-start | bytes 2692
  8.8 5.9 %copy-start = (f32[5,5]{0,1:T(8,128)S(1)}, f32[5,5]{0,1:T(8,128)}, u32[]{:S(2)}) copy-start(f32[5,5]{0,1:T(8,128)} %constant.134.clone) | copy-start | bytes 304
  8.8 5.8 %copy-start.1 = (f32[5,5]{0,1:T(8,128)S(1)}, f32[5,5]{0,1:T(8,128)}, u32[]{:S(2)}) copy-start(f32[5,5]{0,1:T(8,128)} %constant.135.clone) | copy-start | bytes 304
  8.8 8.6 %copy-start.3 = (bf16[224,1152]{1,0:T(8,128)(2,1)S(1)}, bf16[224,1152]{1,0:T(8,128)(2,1)}, u32[]{:S(2)}) copy-start(bf16[224,1152]{1,0:T(8,128)(2,1)} %cm.1) | copy-start | bytes 1548292
  10.8 12.0 %collective-permute-start.7 = (bf16[224,1152]{1,0:T(8,128)(2,1)S(1)}, bf16[224,1152]{1,0:T(8,128)(2,1)S(1)}, u32[]{:S(2)}, u32[]{:S(2)}) collective-permute-start(bf16[224,1152]{1,0:T(8,128)(2,1)S(1)} %copy-done.4), channel_id=1, source_target_pairs={{0,8},{8,0},{32,40},{40,32},{64,72},{72,64},{96,104},{104,96},{128... | collective-permute-start | bytes 1548296 | tf_op jit(solution)/shard_map/ppermute | solution.py:41
  14.5 2.8 %collective-permute-start.6 = (s32[224]{0:T(256)S(1)}, s32[224]{0:T(256)S(1)}, u32[]{:S(2)}, u32[]{:S(2)}) collective-permute-start(s32[224]{0:T(256)S(1)} %copy-done.2), channel_id=1, source_target_pairs={{0,8},{8,0},{32,40},{40,32},{64,72},{72,64},{96,104},{104,96},{128... | collective-permute-start | bytes 2696 | tf_op jit(solution)/shard_map/ppermute | solution.py:41
  17.4 5.4 %collective-permute-start.8 = (bf16[224,1152]{1,0:T(8,128)(2,1)S(1)}, bf16[224,1152]{1,0:T(8,128)(2,1)S(1)}, u32[]{:S(2)}, u32[]{:S(2)}) collective-permute-start(bf16[224,1152]{1,0:T(8,128)(2,1)S(1)} %copy-done.3), channel_id=1, source_target_pairs={{0,8},{8,0},{32,40},{40,32},{64,72},{72,64},{96,104},{104,96},{128... | collective-permute-start | bytes 1548296 | tf_op jit(solution)/shard_map/ppermute | solution.py:41
  19.6 18.8 %copy-start.7 = (bf16[224,1152]{1,0:T(8,128)(2,1)}, bf16[224,1152]{1,0:T(8,128)(2,1)S(1)}, u32[]{:S(2)}) copy-start(bf16[224,1152]{1,0:T(8,128)(2,1)S(1)} %collective-permute-done.sm) | copy-start | bytes 1548292
  19.6 18.8 %collective-permute-start.1 = (bf16[224,1152]{1,0:T(8,128)(2,1)S(1)}, bf16[224,1152]{1,0:T(8,128)(2,1)S(1)}, u32[]{:S(2)}, u32[]{:S(2)}) collective-permute-start(bf16[224,1152]{1,0:T(8,128)(2,1)S(1)} %collective-permute-done.sm), channel_id=1, source_target_pairs={{0,8},{8,0},{32,40},{40,32},{64,72},{72,64},{96,104},{104,96},{128... | collective-permute-start | bytes 1548296 | tf_op jit(solution)/shard_map/ppermute | solution.py:41
  22.3 16.1 %copy-start.5 = (bf16[224,1152]{1,0:T(8,128)(2,1)}, bf16[224,1152]{1,0:T(8,128)(2,1)S(1)}, u32[]{:S(2)}) copy-start(bf16[224,1152]{1,0:T(8,128)(2,1)S(1)} %collective-permute-done.2.fm) | copy-start | bytes 1548292
  22.3 16.1 %collective-permute-start.3 = (bf16[224,1152]{1,0:T(8,128)(2,1)S(1)}, bf16[224,1152]{1,0:T(8,128)(2,1)}, u32[]{:S(2)}, u32[]{:S(2)}) collective-permute-start(bf16[224,1152]{1,0:T(8,128)(2,1)S(1)} %collective-permute-done.2.fm), channel_id=1, source_target_pairs={{0,8},{8,0},{32,40},{40,32},{64,72},{72,64},{96,104},{104,96},{128... | collective-permute-start | bytes 1548296 | tf_op jit(solution)/shard_map/ppermute | solution.py:41
  22.4 16.0 %copy-start.6 = (bf16[224,1152]{1,0:T(8,128)(2,1)}, bf16[224,1152]{1,0:T(8,128)(2,1)S(1)}, u32[]{:S(2)}) copy-start(bf16[224,1152]{1,0:T(8,128)(2,1)S(1)} %collective-permute-done.4.em) | copy-start | bytes 1548292
  22.4 16.0 %collective-permute-start.5 = (bf16[224,1152]{1,0:T(8,128)(2,1)S(1)}, bf16[224,1152]{1,0:T(8,128)(2,1)}, u32[]{:S(2)}, u32[]{:S(2)}) collective-permute-start(bf16[224,1152]{1,0:T(8,128)(2,1)S(1)} %collective-permute-done.4.em), channel_id=1, source_target_pairs={{0,8},{8,0},{32,40},{40,32},{64,72},{72,64},{96,104},{104,96},{128... | collective-permute-start | bytes 1548296 | tf_op jit(solution)/shard_map/ppermute | solution.py:41
  22.8 1.0 copy-start.8
  22.8 0.8 copy-start.10
  38.4 0.8 copy-start.9
  65.3 16.9 %collective-permute-start.10 = (bf16[288,1152]{1,0:T(8,128)(2,1)}, bf16[288,1152]{1,0:T(8,128)(2,1)S(1)}, u32[]{:S(2)}, u32[]{:S(2)}) collective-permute-start(bf16[288,1152]{1,0:T(8,128)(2,1)} %get-tuple-element.26), channel_id=1, source_target_pairs={{0,6},{8,25},{32,38},{40,57},{64,70},{72,89},{96,102},{104,121},{1... | collective-permute-start | bytes 1990664 | tf_op jit(solution)/shard_map/ppermute | solution.py:41
  67.1 15.1 %collective-permute-start.11 = (bf16[288,1152]{1,0:T(8,128)(2,1)}, bf16[288,1152]{1,0:T(8,128)(2,1)S(1)}, u32[]{:S(2)}, u32[]{:S(2)}) collective-permute-start(bf16[288,1152]{1,0:T(8,128)(2,1)} %get-tuple-element.27), channel_id=1, source_target_pairs={{0,4},{8,9},{32,36},{40,41},{64,68},{72,73},{96,100},{104,105},{12... | collective-permute-start | bytes 1990664 | tf_op jit(solution)/shard_map/ppermute | solution.py:41
  68.4 17.4 %collective-permute-start.9 = (bf16[288,1152]{1,0:T(8,128)(2,1)}, bf16[288,1152]{1,0:T(8,128)(2,1)S(1)}, u32[]{:S(2)}, u32[]{:S(2)}) collective-permute-start(bf16[288,1152]{1,0:T(8,128)(2,1)} %get-tuple-element.25), channel_id=1, source_target_pairs={{0,2},{8,24},{32,34},{40,56},{64,66},{72,88},{96,98},{104,120},{12... | collective-permute-start | bytes 1990664 | tf_op jit(solution)/shard_map/ppermute | solution.py:41
  87.3 5.5 %collective-permute-start.12 = (bf16[72,1152]{1,0:T(8,128)(2,1)S(1)}, bf16[72,1152]{1,0:T(8,128)(2,1)S(1)}, u32[]{:S(2)}, u32[]{:S(2)}) collective-permute-start(bf16[72,1152]{1,0:T(8,128)(2,1)S(1)} %get-tuple-element.30), channel_id=1, source_target_pairs={{0,16},{8,10},{32,48},{40,42},{64,80},{72,74},{96,112},{104,106},{... | collective-permute-start | bytes 497672 | tf_op jit(solution)/shard_map/ppermute | solution.py:41
  88.3 5.8 %collective-permute-start.13 = (bf16[72,1152]{1,0:T(8,128)(2,1)S(1)}, bf16[72,1152]{1,0:T(8,128)(2,1)S(1)}, u32[]{:S(2)}, u32[]{:S(2)}) collective-permute-start(bf16[72,1152]{1,0:T(8,128)(2,1)S(1)} %get-tuple-element.32), channel_id=1, source_target_pairs={{0,17},{8,14},{32,49},{40,46},{64,81},{72,78},{96,113},{104,110},{... | collective-permute-start | bytes 497672 | tf_op jit(solution)/shard_map/ppermute | solution.py:41
  90.0 5.7 %collective-permute-start.14 = (bf16[72,1152]{1,0:T(8,128)(2,1)S(1)}, bf16[72,1152]{1,0:T(8,128)(2,1)S(1)}, u32[]{:S(2)}, u32[]{:S(2)}) collective-permute-start(bf16[72,1152]{1,0:T(8,128)(2,1)S(1)} %get-tuple-element.31), channel_id=1, source_target_pairs={{0,1},{8,12},{32,33},{40,44},{64,65},{72,76},{96,97},{104,108},{12... | collective-permute-start | bytes 497672 | tf_op jit(solution)/shard_map/ppermute | solution.py:41
  96.7 13.2 %all-to-all-start = ((bf16[8,81,128]{2,1,0:T(8,128)(2,1)}), bf16[8,81,128]{2,1,0:T(8,128)(2,1)S(1)}, u32[]{:S(2)}, u32[]{:S(2)}) async-start(bf16[8,81,128]{2,1,0:T(8,128)(2,1)} %reshape.75), calls=%async_computation | async-start | bytes 360448 | tf_op jit(solution)/shard_map/all_to_all | solution.py:425
  109.9 6.8 %collective-permute-start.15 = (f32[81,128]{1,0:T(8,128)S(1)}, f32[81,128]{1,0:T(8,128)S(1)}, u32[]{:S(2)}, u32[]{:S(2)}) collective-permute-start(f32[81,128]{1,0:T(8,128)S(1)} %convert_reduce_fusion), channel_id=1, source_target_pairs={{0,1},{8,0},{32,33},{40,32},{64,65},{72,64},{96,97},{104,96},{128,... | collective-permute-start | bytes 124424 | tf_op jit(solution)/shard_map/ppermute | solution.py:41
  113.4 6.9 %collective-permute-start.16 = (f32[81,128]{1,0:T(8,128)S(1)}, f32[81,128]{1,0:T(8,128)S(1)}, u32[]{:S(2)}, u32[]{:S(2)}) collective-permute-start(f32[81,128]{1,0:T(8,128)S(1)} %convert_reduce_fusion), channel_id=1, source_target_pairs={{8,1},{40,33},{72,65},{104,97},{136,129},{168,161},{200,193},{232,... | collective-permute-start | bytes 124424 | tf_op jit(solution)/shard_map/ppermute | solution.py:41
  120.5 5.5 %collective-permute-start.17 = (f32[2,81,128]{2,0,1:T(2,128)S(1)}, f32[2,81,128]{2,0,1:T(2,128)S(1)}, u32[]{:S(2)}, u32[]{:S(2)}) collective-permute-start(f32[2,81,128]{2,0,1:T(2,128)S(1)} %get-tuple-element.36), channel_id=1, source_target_pairs={{0,2},{8,10},{32,34},{40,42},{64,66},{72,74},{96,98},{104,106},{12... | collective-permute-start | bytes 248840 | tf_op jit(solution)/shard_map/ppermute | solution.py:41
  120.6 5.4 %collective-permute-start.18 = (f32[2,81,128]{2,0,1:T(2,128)S(1)}, f32[2,81,128]{2,0,1:T(2,128)S(1)}, u32[]{:S(2)}, u32[]{:S(2)}) collective-permute-start(f32[2,81,128]{2,0,1:T(2,128)S(1)} %get-tuple-element.36), channel_id=1, source_target_pairs={{0,4},{8,12},{32,36},{40,44},{64,68},{72,76},{96,100},{104,108},{1... | collective-permute-start | bytes 248840 | tf_op jit(solution)/shard_map/ppermute | solution.py:41
  122.3 4.2 %collective-permute-start.19 = (f32[2,81,128]{2,0,1:T(2,128)S(1)}, f32[2,81,128]{2,0,1:T(2,128)S(1)}, u32[]{:S(2)}, u32[]{:S(2)}) collective-permute-start(f32[2,81,128]{2,0,1:T(2,128)S(1)} %get-tuple-element.36), channel_id=1, source_target_pairs={{0,6},{8,14},{32,38},{40,46},{64,70},{72,78},{96,102},{104,110},{1... | collective-permute-start | bytes 248840 | tf_op jit(solution)/shard_map/ppermute | solution.py:41
where the time goes:
time: 130 us
  Pallas kernels  40.7 us (31%)
  waiting for transfers between devices  37.3 us (29%)
  starting transfers between devices  36.7 us (28%)
  other arithmetic  6.37 us (5%)
  local copies, waits for them, and re-layouts  6.12 us (5%)
  between operations  2.92 us (2%)
    ppermute x20, starting transfers between devices, moved(): return lax.ppermute(value, AXES, pairs)  32.1 us
    ppermute x20, waiting for transfers between devices, moved(): return lax.ppermute(value, AXES, pairs)  28.7 us
    pallas_call x1, Pallas kernels, arrived_part(): pl.pallas_call(arrived_kernel, out_shape=[jax.ShapeDtypeStruct((D // 4, D...  26.1 us
    pallas_call x1, Pallas kernels, own_part(): pl.pallas_call(own_kernel, out_shape=[jax.ShapeDtypeStruct((2 * R, D), BF...  14.6 us
    all_to_all x1, waiting for transfers between devices, local(): three = lax.all_to_all(two, AXES, 0, 0, axis_index_groups=ALONG_Z)  8.55 us
    all_to_all x1, starting transfers between devices, local(): three = lax.all_to_all(two, AXES, 0, 0, axis_index_groups=ALONG_Z)  4.65 us
  transfers between devices with their start and end apart: 21, of which 10 were waited for; matrix products, arithmetic and copies ran while one was open for 3% of the time, Pallas kernels for 11%

commit v1 on v0

--- a/solution.py
+++ b/solution.py
@@ -85,6 +85,12 @@
 THIRDS = [(n, 384) for n in range(0, D, 384)]
 
 
+IMAGE_AT = np.array([[0, 1, 4, 5, 100], [2, 3, -2, -1, 6]])
+CAPTION_AT = np.array([[0, 1, 2, 3], [2, 3, 0, 1]])
+APART = CAPTION_AT[:, None, :] - IMAGE_AT[:, :, None]
+TAKEN = ((APART >= -3) & (APART <= 2)).astype(float).tolist()
+
+
 def nt_dot(a, b):
     return lax.dot_general(a, b, (((1,), (1,)), ((), ())), preferred_element_type=F32)
 
@@ -95,15 +101,15 @@
     return copy
 
 
-def by_role(core_ref, choices, sems):
+def by_role(place_ref, choices, sems):
     waits = []
     for k, (zero, one, dst) in enumerate(choices):
 
-        @pl.when(core_ref[0] == 0)
+        @pl.when(place_ref[0] == 0)
         def _():
             fetch(zero, dst, sems.at[k])
 
-        @pl.when(core_ref[0] == 1)
+        @pl.when(place_ref[0] == 1)
         def _():
             fetch(one, dst, sems.at[k])
 
@@ -120,49 +126,73 @@
     return lax.rsqrt(squares + 1e-6)
 
 
-def pair_weights(scal_ref, rows, cols, xs, height, ys, gs, signs=None):
-    logits = nt_dot(rows, cols) * scal_ref[0] + scal_ref[1]
+def pair_weights(scalars, rows, cols, xs, height, ys, scale_of, gs, label=None):
+    sharpness, shift = scalars
+    logits = nt_dot(rows, cols) * sharpness + shift
     for i, x in enumerate(xs):
         for j, y in enumerate(ys):
             part = logits[i * height : (i + 1) * height, j * PAD : (j + 1) * PAD]
-            scale = scal_ref[2 + x * 5 + y]
-            if signs is not None and x == y:
-                sign = signs[x]
-                g = (scale * sign) * jax.nn.sigmoid(sign * part)
+            scale = scale_of(x, y)
+            if label is not None and x == y:
+                match = label(x)
+                g = jnp.where(match, -scale, scale) * jax.nn.sigmoid(jnp.where(match, -part, part))
             else:
                 g = scale * jax.nn.sigmoid(part)
             gs[i * height : (i + 1) * height, j * PAD : (j + 1) * PAD] = g.astype(BF16)
 
 
 def own_kernel(
-    core_ref, scal_ref, lab_ref, im, io, cm, co, wi, wc, order,
-    zx, zy, ux, ix, ft, dz,
-    f, w, pv, lab, tmp, gs, sems,
+    place_ref, sharp_ref, shift_ref, coef_ref, mine_c, other_c, mine_r, other_r, im, io, cm, co, wi, wc, order,
+    zx_out, zy_out, ux_out, ix_out, ft_out, dz_out,
+    f, w, pv, tmp, zx, zy, ux, ix, gs, ft, dz, sems,
 ):
-    waits = by_role(
-        core_ref,
-        [
-            (im, co, f.at[0, pl.ds(0, R)]), (io, cm, f.at[0, pl.ds(R, R)]),
-            (cm, io, f.at[1, pl.ds(0, R)]), (co, im, f.at[1, pl.ds(R, R)]),
-            (wi, wc, w.at[0]), (wc, wi, w.at[1]),
-        ],
-        sems,
-    )
-    late = [fetch(order, pv, sems.at[6]), fetch(lab_ref, lab, sems.at[7])]
-    for wait in waits:
+    core = place_ref[0]
+    first = by_role(
+        place_ref, [(im, co, f.at[0, pl.ds(0, R)]), (io, cm, f.at[0, pl.ds(R, R)]), (wi, wc, w.at[0])],
+        sems.at[pl.ds(0, 3)],
+    )
+    second = by_role(
+        place_ref, [(cm, io, f.at[1, pl.ds(0, R)]), (co, im, f.at[1, pl.ds(R, R)]), (wc, wi, w.at[1])],
+        sems.at[pl.ds(3, 3)],
+    )
+    for wait in first:
         wait.wait()
     inv = project(f[0], w.at[0], tmp, 2 * R)
     ix[...] = jnp.broadcast_to(inv, (2 * R, 128))
-    for n, wd in THIRDS:
-        unit = tmp[:, n : n + wd] * inv
-        ux[:, n : n + wd] = unit
-        zx[:, n : n + wd] = unit.astype(BF16)
+    unit = tmp[...] * inv
+    ux[...] = unit
+    zx[...] = unit.astype(BF16)
+    outs = [fetch(ux, ux_out, sems.at[6]), fetch(zx, zx_out, sems.at[7]), fetch(ix, ix_out, sems.at[8])]
+    for wait in second:
+        wait.wait()
+    late = fetch(order, pv, sems.at[9])
     inv = project(f[1], w.at[1], tmp, 2 * R)
     for b in range(2):
         zy[b * PAD : b * PAD + R] = (tmp[b * R : (b + 1) * R] * inv[b * R : (b + 1) * R]).astype(BF16)
         zy[b * PAD + R : (b + 1) * PAD] = jnp.zeros((PAD - R, D), BF16)
-    for copy in late:
-        copy.wait()
+    outs.append(fetch(zy, zy_out, sems.at[10]))
+
+    def label(k):
+        mine = core == k
+        by_col = jnp.where(mine, mine_c[...], other_c[...])
+        by_row = jnp.where(mine, mine_r[...], other_r[...])
+        shape = (R, PAD)
+        target = jnp.where(core == 0, jnp.broadcast_to(by_col, shape), jnp.broadcast_to(by_row, shape))
+        place = jnp.where(
+            core == 0, lax.broadcasted_iota(jnp.int32, shape, 1), lax.broadcasted_iota(jnp.int32, shape, 0)
+        )
+        return place == target
+
+    scalars = (sharp_ref[0], shift_ref[0])
+    pair_weights(scalars, zx[...], zy[...], (0, 1), R, (0, 1), lambda x, y: coef_ref[0], gs, label)
+
+    @pl.loop(0, 3)
+    def _(k):
+        cols = pl.ds(pl.multiple_of(k * 384, 384), 384)
+        dz[:, cols] = sharp_ref[0] * jnp.dot(gs[...], zy[:, cols], preferred_element_type=F32)
+
+    outs.append(fetch(dz, dz_out, sems.at[11]))
+    late.wait()
 
     @pl.loop(0, 3)
     def _(k):
@@ -170,57 +200,58 @@
         ft[rows, 0 : 2 * R] = nt_dot(pv[rows], f[0]).astype(BF16)
 
     ft[:, 2 * R :] = jnp.zeros((D, 2 * PAD - 2 * R), BF16)
-    pair_weights(scal_ref, zx[...], zy[...], (0, 1), R, (0, 1), gs, lab)
-
-    @pl.loop(0, 3)
-    def _(k):
-        cols = pl.ds(pl.multiple_of(k * 384, 384), 384)
-        dz[:, cols] = scal_ref[0] * jnp.dot(gs[...], zy[:, cols], preferred_element_type=F32)
-
-
-def own_part(core, scal, lab, im, io, cm, co, wi, wc, order):
+    for copy in outs + [fetch(ft, ft_out, sems.at[12])]:
+        copy.wait()
+
+
+def own_part(place, sharp, shift, coef, mine_c, other_c, mine_r, other_r, *operands):
     smem = pl.BlockSpec(memory_space=pltpu.SMEM)
     vmem = pl.BlockSpec(memory_space=pltpu.VMEM)
+    hbm = pl.BlockSpec(memory_space=pl.ANY)
+    results = [
+        ((2 * R, D), BF16), ((2 * PAD, D), BF16), ((2 * R, D), F32), ((2 * R, 128), F32), ((D, 2 * PAD), BF16),
+        ((2 * R, D), F32),
+    ]
     return pl.pallas_call(
         own_kernel,
-        out_shape=[
-            jax.ShapeDtypeStruct((2 * R, D), BF16),
-            jax.ShapeDtypeStruct((2 * PAD, D), BF16),
-            jax.ShapeDtypeStruct((2 * R, D), F32),
-            jax.ShapeDtypeStruct((2 * R, 128), F32),
-            jax.ShapeDtypeStruct((D, 2 * PAD), BF16),
-            jax.ShapeDtypeStruct((2 * R, D), F32),
-        ],
-        in_specs=[smem, smem] + [pl.BlockSpec(memory_space=pl.ANY)] * 8,
-        out_specs=[vmem] * 6,
+        out_shape=[jax.ShapeDtypeStruct(*result) for result in results],
+        in_specs=[smem] * 4 + [vmem] * 4 + [hbm] * 7,
+        out_specs=[hbm] * 6,
         scratch_shapes=[
             pltpu.VMEM((2, 2 * R, D), BF16),
             pltpu.VMEM((2, D, D), BF16),
             pltpu.VMEM((D, D), BF16),
-            pltpu.VMEM((2, R, PAD), F32),
             pltpu.VMEM((2 * R, D), F32),
+            pltpu.VMEM((2 * R, D), BF16),
+            pltpu.VMEM((2 * PAD, D), BF16),
+            pltpu.VMEM((2 * R, D), F32),
+            pltpu.VMEM((2 * R, 128), F32),
             pltpu.VMEM((2 * R, 2 * PAD), BF16),
-            pltpu.SemaphoreType.DMA((8,)),
+            pltpu.VMEM((D, 2 * PAD), BF16),
+            pltpu.VMEM((2 * R, D), F32),
+            pltpu.SemaphoreType.DMA((13,)),
         ],
         compiler_params=pltpu.CompilerParams(vmem_limit_bytes=60 * 2**20),
-        cost_estimate=pl.CostEstimate(flops=6 * 10**9, bytes_accessed=16 * 10**6, transcendentals=230000),
-    )(core, scal, lab, im, io, cm, co, wi, wc, order)
+        cost_estimate=pl.CostEstimate(flops=6 * 10**9, bytes_accessed=16 * 10**6, transcendentals=500000),
+    )(place, sharp, shift, coef, mine_c, other_c, mine_r, other_r, *operands)
 
 
 def arrived_kernel(
-    core_ref, scal_ref, sm, so, fm, fo, em, eo, wi, wc, order, zx_in, zy_in, ux_in, ix_in, ft_in, dz_in,
+    place_ref, sharp_ref, shift_ref, coef_ref,
+    sm, so, fm, fo, em, eo, wi, wc, order, zx_in, zy_in, ux_in, ix_in, ft_in, dz_in,
     out0, out1, out2, out3,
     f, w, pv, zx, z, uo, ua, io_, ia, fto, fta, dz, da, gs, dp, tmp, sems,
 ):
-    role = core_ref[0]
+    role, y_lo = place_ref[0], place_ref[1]
+    scalars = (sharp_ref[0], shift_ref[0])
     gap = PAD - R
     rows_first = by_role(
-        core_ref,
+        place_ref,
         [(fm, so, f.at[0, pl.ds(0, R)]), (fo, sm, f.at[1, pl.ds(0, R)]), (wi, wc, w.at[0])],
         sems.at[pl.ds(0, 3)],
     )
     cols_next = by_role(
-        core_ref,
+        place_ref,
         [(sm, fo, f.at[3, pl.ds(0, R)]), (so, fm, f.at[4, pl.ds(0, R)]), (wc, wi, w.at[1])],
         sems.at[pl.ds(3, 3)],
     )
@@ -249,8 +280,8 @@
     extra = pltpu.make_async_copy(em, f.at[2, pl.ds(0, R)], sems.at[6])
     for wait in rows_first + [extra]:
         wait.wait()
+    order_copy = fetch(order, pv, sems.at[7])
     late = [
-        fetch(order, pv, sems.at[7]),
         fetch(zx_in, zx, sems.at[8]),
         fetch(zy_in, z.at[pl.ds(3 * PAD, 2 * PAD)], sems.at[9]),
         fetch(ux_in, uo, sems.at[10]),
@@ -276,19 +307,21 @@
         inv = project(f[k + 3, 0:R], w.at[1], tmp, R)
         z[pl.ds(pl.multiple_of((k + 5) * PAD, PAD), R)] = (tmp[...] * inv).astype(BF16)
 
+    order_copy.wait()
+
+    @pl.loop(0, 3)
+    def _(k):
+        rows = pl.ds(pl.multiple_of(k * 384, 384), 384)
+        fta[rows] = nt_dot(pv[rows], f[0:3].reshape(3 * PAD, D)).astype(BF16)
+
     for copy in late:
         copy.wait()
-
-    @pl.loop(0, 3)
-    def _(k):
-        rows = pl.ds(pl.multiple_of(k * 384, 384), 384)
-        fta[rows] = nt_dot(pv[rows], f[0:3].reshape(3 * PAD, D)).astype(BF16)
 
     def spread(m, cols, y0, y1, kept, unit, inverse, base):
         @pl.loop(0, 3)
         def _(k):
             at = pl.ds(pl.multiple_of(k * 384, 384), 384)
-            d = scal_ref[0] * jnp.dot(gs[0:m, 0:cols], z[y0 * PAD : y1 * PAD, at], preferred_element_type=F32)
+            d = sharp_ref[0] * jnp.dot(gs[0:m, 0:cols], z[y0 * PAD : y1 * PAD, at], preferred_element_type=F32)
             if kept:
                 d = d + dz[:, at]
             da[0:m, at] = d
@@ -296,20 +329,29 @@
         along = jnp.sum(da[0:m] * unit[0:m], axis=1, keepdims=True)
         dp[base : base + m] = ((da[0:m] - unit[0:m] * along) * inverse[0:m, 0:1]).astype(BF16)
 
+    def scale(image, caption):
+        return coef_ref[0] * jnp.where(y_lo == 0, TAKEN[0][image][caption], TAKEN[1][image][caption])
+
+    def by_image(x, y):
+        return scale(x, y)
+
+    def by_caption(x, y):
+        return scale(y, x)
+
     @pl.when(role == 0)
     def _():
-        pair_weights(scal_ref, zx[...], z[5 * PAD : 7 * PAD], (0, 1), R, (2, 3), gs)
+        pair_weights(scalars, zx[...], z[5 * PAD : 7 * PAD], (0, 1), R, (2, 3), by_image, gs)
         spread(2 * R, 2 * PAD, 5, 7, True, uo, io_, 0)
-        pair_weights(scal_ref, z[0 : 2 * PAD], z[4 * PAD : 7 * PAD], (2, 3), PAD, (1, 2, 3), gs)
+        pair_weights(scalars, z[0 : 2 * PAD], z[4 * PAD : 7 * PAD], (2, 3), PAD, (1, 2, 3), by_image, gs)
         spread(2 * PAD, 3 * PAD, 4, 7, False, ua, ia, 2 * PAD)
-        pair_weights(scal_ref, z[2 * PAD : 3 * PAD], z[4 * PAD : 5 * PAD], (4,), PAD, (1,), gs)
+        pair_weights(scalars, z[2 * PAD : 3 * PAD], z[4 * PAD : 5 * PAD], (4,), PAD, (1,), by_image, gs)
         spread(PAD, PAD, 4, 5, False, ua.at[2 * PAD : 3 * PAD], ia.at[2 * PAD : 3 * PAD], 4 * PAD)
 
     @pl.when(role == 1)
     def _():
-        pair_weights(scal_ref, zx[...], z[5 * PAD : 8 * PAD], (0, 1), R, (2, 3, 4), gs)
+        pair_weights(scalars, zx[...], z[5 * PAD : 8 * PAD], (0, 1), R, (2, 3, 4), by_caption, gs)
         spread(2 * R, 3 * PAD, 5, 8, True, uo, io_, 0)
-        pair_weights(scal_ref, z[0 : 2 * PAD], z[3 * PAD : 7 * PAD], (2, 3), PAD, (0, 1, 2, 3), gs)
+        pair_weights(scalars, z[0 : 2 * PAD], z[3 * PAD : 7 * PAD], (2, 3), PAD, (0, 1, 2, 3), by_caption, gs)
         spread(2 * PAD, 4 * PAD, 3, 7, False, ua, ia, 2 * PAD)
         dp[4 * PAD : 5 * PAD] = jnp.zeros((PAD, D), BF16)
 
@@ -326,13 +368,13 @@
             ).astype(BF16)
 
 
-def arrived_part(core, scal, *operands):
+def arrived_part(place, sharp, shift, coef, *operands):
     smem = pl.BlockSpec(memory_space=pltpu.SMEM)
     vmem = pl.BlockSpec(memory_space=pltpu.VMEM)
     return pl.pallas_call(
         arrived_kernel,
         out_shape=[jax.ShapeDtypeStruct((D // 4, D), BF16)] * 4,
-        in_specs=[smem, smem] + [pl.BlockSpec(memory_space=pl.ANY)] * 15,
+        in_specs=[smem] * 4 + [pl.BlockSpec(memory_space=pl.ANY)] * 15,
         out_specs=[vmem] * 4,
         scratch_shapes=[
             pltpu.VMEM((6, PAD, D), BF16),
@@ -355,7 +397,7 @@
         ],
         compiler_params=pltpu.CompilerParams(vmem_limit_bytes=60 * 2**20),
         cost_estimate=pl.CostEstimate(flops=14 * 10**9, bytes_accessed=20 * 10**6, transcendentals=800000),
-    )(core, scal, *operands)
+    )(place, sharp, shift, coef, *operands)
 
 
 def local(
@@ -372,48 +414,37 @@
     core, y_lo = place % 2, (place // 2) % 2
     x, y_hi = lax.axis_index("replica") // 2, lax.axis_index("replica") % 2
     y = y_hi * 2 + y_lo
-    coefficient = objective_multiplier[0] / (lax.axis_size("dp") * R)
-
-    cap_sib = swap_chips(text_encoder_features)
-    img_far = image_to_neighbour(picture_encoder_features)
-    img_extra = image_down(picture_encoder_features)
+    role = jnp.stack([core, y_lo, x, y]).astype(jnp.int32)
+    coefficient = objective_multiplier / (lax.axis_size("dp") * R)
+
+    own_img = swap_cores(picture_encoder_features)
+    own_cap = swap_cores(text_encoder_features)
     target_other = swap_cores(matching_target)
+    cap, img, coefficient = lax.optimization_barrier(
+        (text_encoder_features, picture_encoder_features, coefficient)
+    )
+    cap_sib = swap_chips(cap)
+    img_far = image_to_neighbour(img)
+    img_extra = image_down(img)
+
+    def wide(target):
+        return jnp.pad(target, (0, PAD - R), constant_values=-1)[None]
+
+    order = row_order(core, x, y).astype(jnp.int32)
+    one_hot = (lax.broadcasted_iota(jnp.int32, (D, D), 1) == order[:, None]).astype(BF16)
+    kept = own_part(
+        role, sharpness_param, offset_shift, coefficient,
+        matching_target[:, None], target_other[:, None], wide(matching_target), wide(target_other),
+        picture_encoder_features, own_img, text_encoder_features, own_cap,
+        picture_projector, text_projector, one_hot,
+    )
+    cap_sib, img_far, img_extra, kept = lax.optimization_barrier((cap_sib, img_far, img_extra, kept))
     cap_sib_other = swap_cores(cap_sib)
     img_far_other = swap_cores(img_far)
     img_extra_other = swap_cores(img_extra)
-
-    even = y_lo == 0
-    img_at = np.array([[0, 1, 4, 5, 100], [2, 3, -2, -1, 6]])
-    cap_at = np.array([[0, 1, 2, 3], [2, 3, 0, 1]])
-    apart = cap_at[:, None, :] - img_at[:, :, None]
-    taken = np.pad(((apart >= -3) & (apart <= 2)).astype(np.float32), ((0, 0), (0, 0), (0, 1)))
-    first = core == 0
-    taken = jnp.where(even, taken[0], taken[1])
-    scales = coefficient * jnp.where(first, taken, taken.T)
-    scalars = jnp.concatenate([sharpness_param, offset_shift, scales.reshape(-1)])
-    targets = jnp.stack(
-        [jnp.where(first, matching_target, target_other), jnp.where(first, target_other, matching_target)]
-    )
-    column = lax.broadcasted_iota(jnp.int32, (2, R, PAD), 2)
-    row = lax.broadcasted_iota(jnp.int32, (2, R, PAD), 1)
-    wide = jnp.pad(targets, ((0, 0), (0, PAD - R)), constant_values=-1)
-    match = jnp.where(first, column == targets[:, :, None], row == wide[:, None, :])
-    signs = jnp.where(match, -1.0, 1.0).astype(F32)
-    order = row_order(core, x, y).astype(jnp.int32)
-    one_hot = (lax.broadcasted_iota(jnp.int32, (D, D), 1) == order[:, None]).astype(BF16)
-
-    role = core[None].astype(jnp.int32)
-    img, cap, one_hot = lax.optimization_barrier(
-        (picture_encoder_features, text_encoder_features, one_hot)
-    )
-    own_img = swap_cores(img)
-    own_cap = swap_cores(cap)
-    kept = own_part(
-        role, scalars, signs, picture_encoder_features, own_img, text_encoder_features, own_cap,
-        picture_projector, text_projector, one_hot,
-    )
     parts = arrived_part(
-        role, scalars, cap_sib, cap_sib_other, img_far, img_far_other, img_extra, img_extra_other,
+        role, sharpness_param, offset_shift, coefficient,
+        cap_sib, cap_sib_other, img_far, img_far_other, img_extra, img_extra_other,
         picture_projector, text_projector, one_hot, *kept,
     )
 
@@ -425,6 +456,7 @@
     three = lax.all_to_all(two, AXES, 0, 0, axis_index_groups=ALONG_Z)
     mine = jnp.sum(three.astype(F32), axis=0)
 
+    first = core == 0
     ring, cross = pass_on(mine), pass_across(mine)
     home = core == y_hi
     image_piece = jnp.where(home & first, mine, jnp.where(home | first, ring, cross))

time: 130 us -> 132 us (1.015)
  local copies, waits for them, and re-layouts: 6.12 us -> 8.76 us
  Pallas kernels: 40.7 us -> 38.7 us
  waiting for transfers between devices: 37.3 us -> 38.9 us
    pallas_call x1, Pallas kernels: 14.6 us -> 12.6 us  [own_part(): pl.pallas_call(own_kernel, out_shape=[jax.ShapeDtypeStruct(*result) for r...]
    ppermute x20, waiting for transfers between devices: 28.7 us -> 30.5 us  [moved(): return lax.ppermute(value, AXES, pairs)]
    broadcast_in_dim x0 -> x2, local copies, waits for them, and re-layouts: none -> 1.56 us  [the longest x1 0.78 us: local(): matching_target[:, None]]
  transfers between devices with their start and end apart: 21 -> 21, of which waited for: 10 -> 13; matrix products, arithmetic and copies ran while one was open for 3% -> 5% of each run, Pallas kernels for 11% -> 10%
where the time goes in v1:
time: 132 us; the launch traced here: 131 us
  waiting for transfers between devices  38.9 us (29%)
  Pallas kernels  38.7 us (29%)
  starting transfers between devices  36.9 us (28%)
  local copies, waits for them, and re-layouts  8.76 us (7%)
  other arithmetic  5.42 us (4%)
  between operations  2.82 us (2%)
    ppermute x20, starting transfers between devices, moved(): return lax.ppermute(value, AXES, pairs)  31.3 us
    ppermute x20, waiting for transfers between devices, moved(): return lax.ppermute(value, AXES, pairs)  30.5 us
    pallas_call x1, Pallas kernels, arrived_part(): pl.pallas_call(arrived_kernel, out_shape=[jax.ShapeDtypeStruct((D // 4, D...  26.1 us
    pallas_call x1, Pallas kernels, own_part(): pl.pallas_call(own_kernel, out_shape=[jax.ShapeDtypeStruct(*result) for r...  12.6 us
    all_to_all x1, waiting for transfers between devices, local(): three = lax.all_to_all(two, AXES, 0, 0, axis_index_groups=ALONG_Z)  8.44 us
    all_to_all x1, starting transfers between devices, local(): three = lax.all_to_all(two, AXES, 0, 0, axis_index_groups=ALONG_Z)  5.54 us
  transfers between devices with their start and end apart: 21, of which 13 were waited for; matrix products, arithmetic and copies ran while one was open for 5% of the time, Pallas kernels for 10%

profile of v1, /device:TPU:1, one launch (start us, length us, event | category | flops | bytes accessed | tf_op | source)
XLA Modules:
  0.0 131.5 jit_solution(17885436251228464642)
XLA Ops:
  0.6 3.3 %collective-permute-start.4 = (bf16[224,1152]{1,0:T(8,128)(2,1)}, bf16[224,1152]{1,0:T(8,128)(2,1)S(1)}, u32[]{:S(2)}, u32[]{:S(2)}) collective-permute-start(bf16[224,1152]{1,0:T(8,128)(2,1)} %im.1), channel_id=1, source_target_pairs={{0,8},{8,0},{32,40},{40,32},{64,72},{72,64},{96,104},{104,96},{128... | collective-permute-start | bytes 1548296 | tf_op jit(solution)/shard_map/ppermute | solution.py:41
  4.7 3.9 %collective-permute-start.1 = (bf16[224,1152]{1,0:T(8,128)(2,1)}, bf16[224,1152]{1,0:T(8,128)(2,1)S(1)}, u32[]{:S(2)}, u32[]{:S(2)}) collective-permute-start(bf16[224,1152]{1,0:T(8,128)(2,1)} %im.1), channel_id=1, source_target_pairs={{0,224},{8,232},{32,0},{40,8},{64,32},{72,40},{96,64},{104,72},{12... | collective-permute-start | bytes 1548296 | tf_op jit(solution)/shard_map/ppermute | solution.py:41
  10.9 2.0 %fusion.order = bf16[1152,1152]{1,0:T(8,128)(2,1)} fusion(s32[1152]{0:T(1024)S(1)} %fusion.6), kind=kLoop, calls=%fused_computation.2 | loop fusion | flops 2654208 | bytes 2658816 | tf_op jit(solution)/shard_map/convert_element_type | solution.py:434
  16.2 2.6 %collective-permute-start = (bf16[224,1152]{1,0:T(8,128)(2,1)S(1)}, bf16[224,1152]{1,0:T(8,128)(2,1)S(1)}, u32[]{:S(2)}, u32[]{:S(2)}) collective-permute-start(bf16[224,1152]{1,0:T(8,128)(2,1)S(1)} %copy-done.1), channel_id=1, source_target_pairs={{0,16},{8,24},{32,48},{40,56},{64,80},{72,88},{96,112},{104,120},{... | collective-permute-start | bytes 1548296 | tf_op jit(solution)/shard_map/ppermute | solution.py:41
  20.1 0.8 copy-done.4
  21.1 12.6 %shard_map.131 = (bf16[448,1152]{1,0:T(8,128)(2,1)}, bf16[512,1152]{1,0:T(8,128)(2,1)}, f32[448,1152]{1,0:T(8,128)}, f32[448,128]{1,0:T(8,128)}, bf16[1152,512]{1,0:T(8,128)(2,1)}, /*index=5*/f32[448,1152]{1,0:T(8,128)}) custom-call(s32[4]{0:T(128)} %pad_add_fusion.place_ref, f32[1]{0:T(128)S(6)} %copy.17.sharp_ref, f32[1]{0:T(128)S(6)} %copy.18.shift_ref, ...), custom_call_target="tpu_custom_call" | custom-call | flops 6000000000 | bytes 16000000 | tf_op jit(solution)/shard_map/pallas_call | solution.py:215
  34.7 1.1 collective-permute-done.6.so
  37.2 0.8 copy-done.9
  38.1 26.1 %shard_map.132 = (bf16[288,1152]{1,0:T(8,128)(2,1)}, bf16[288,1152]{1,0:T(8,128)(2,1)}, bf16[288,1152]{1,0:T(8,128)(2,1)}, bf16[288,1152]{1,0:T(8,128)(2,1)}) custom-call(s32[4]{0:T(128)} %pad_add_fusion.place_ref, f32[1]{0:T(128)S(6)} %copy.17.sharp_ref, f32[1]{0:T(128)S(6)} %copy.18.shift_ref, f32[1]{0:T(128)S(6)} %div.34.coef_ref, ...), custom_call_target="tpu_custom_call" | custom-call | flops 14000000000 | bytes 20000000 | tf_op jit(solution)/shard_map/pallas_call | solution.py:374
  64.2 1.5 %collective-permute-start.10 = (bf16[288,1152]{1,0:T(8,128)(2,1)}, bf16[288,1152]{1,0:T(8,128)(2,1)S(1)}, u32[]{:S(2)}, u32[]{:S(2)}) collective-permute-start(bf16[288,1152]{1,0:T(8,128)(2,1)} %get-tuple-element.44), channel_id=1, source_target_pairs={{0,6},{8,25},{32,38},{40,57},{64,70},{72,89},{96,102},{104,121},{1... | collective-permute-start | bytes 1990664 | tf_op jit(solution)/shard_map/ppermute | solution.py:41
  65.7 1.3 collective-permute-start.11
  67.8 6.5 %collective-permute-done.10 = bf16[288,1152]{1,0:T(8,128)(2,1)S(1)} collective-permute-done((bf16[288,1152]{1,0:T(8,128)(2,1)}, bf16[288,1152]{1,0:T(8,128)(2,1)S(1)}, u32[]{:S(2)}, u32[]{:S(2)}) %collective-permute-start.10) | collective-permute-done | bytes 663584 | tf_op jit(solution)/shard_map/ppermute | solution.py:41
  74.3 3.0 %collective-permute-done.11 = bf16[288,1152]{1,0:T(8,128)(2,1)S(1)} collective-permute-done((bf16[288,1152]{1,0:T(8,128)(2,1)}, bf16[288,1152]{1,0:T(8,128)(2,1)S(1)}, u32[]{:S(2)}, u32[]{:S(2)}) %collective-permute-start.11) | collective-permute-done | bytes 663584 | tf_op jit(solution)/shard_map/ppermute | solution.py:41
  77.3 7.1 %collective-permute-done.9 = bf16[288,1152]{1,0:T(8,128)(2,1)S(1)} collective-permute-done((bf16[288,1152]{1,0:T(8,128)(2,1)}, bf16[288,1152]{1,0:T(8,128)(2,1)S(1)}, u32[]{:S(2)}, u32[]{:S(2)}) %collective-permute-start.9) | collective-permute-done | bytes 663584 | tf_op jit(solution)/shard_map/ppermute | solution.py:41
  84.4 1.4 %add_convert_fusion = bf16[288,1152]{1,0:T(8,128)(2,1)S(1)} fusion(bf16[288,1152]{1,0:T(8,128)(2,1)S(1)} %collective-permute-done.11, bf16[288,1152]{1,0:T(8,128)(2,1)S(1)} %collective-permute-done.10, bf16[288,1152]{1,0:T(8,128)(2,1)S(1)} %collective-permute-done.9, bf16[288,1152]{1,0:T(8,128)(2,1)} %get-tuple-element.42), kind=kLoop, calls=%fused_computation.3 | loop fusion | flops 2654208 | bytes 3317760 | tf_op jit(solution)/shard_map/convert_element_type | solution.py:452
  85.8 1.0 collective-permute-start.12
  86.8 1.8 %collective-permute-start.13 = (bf16[72,1152]{1,0:T(8,128)(2,1)S(1)}, bf16[72,1152]{1,0:T(8,128)(2,1)S(1)}, u32[]{:S(2)}, u32[]{:S(2)}) collective-permute-start(bf16[72,1152]{1,0:T(8,128)(2,1)S(1)} %get-tuple-element.50), channel_id=1, source_target_pairs={{0,17},{8,14},{32,49},{40,46},{64,81},{72,78},{96,113},{104,110},{... | collective-permute-start | bytes 497672 | tf_op jit(solution)/shard_map/ppermute | solution.py:41
  88.6 1.2 collective-permute-start.14
  89.8 1.5 %collective-permute-done.12 = bf16[72,1152]{1,0:T(8,128)(2,1)S(1)} collective-permute-done((bf16[72,1152]{1,0:T(8,128)(2,1)S(1)}, bf16[72,1152]{1,0:T(8,128)(2,1)S(1)}, u32[]{:S(2)}, u32[]{:S(2)}) %collective-permute-start.12) | collective-permute-done | bytes 165920 | tf_op jit(solution)/shard_map/ppermute | solution.py:41
  91.3 1.3 %collective-permute-done.13 = bf16[72,1152]{1,0:T(8,128)(2,1)S(1)} collective-permute-done((bf16[72,1152]{1,0:T(8,128)(2,1)S(1)}, bf16[72,1152]{1,0:T(8,128)(2,1)S(1)}, u32[]{:S(2)}, u32[]{:S(2)}) %collective-permute-start.13) | collective-permute-done | bytes 165920 | tf_op jit(solution)/shard_map/ppermute | solution.py:41
  92.7 1.6 %collective-permute-done.14 = bf16[72,1152]{1,0:T(8,128)(2,1)S(1)} collective-permute-done((bf16[72,1152]{1,0:T(8,128)(2,1)S(1)}, bf16[72,1152]{1,0:T(8,128)(2,1)S(1)}, u32[]{:S(2)}, u32[]{:S(2)}) %collective-permute-start.14) | collective-permute-done | bytes 165920 | tf_op jit(solution)/shard_map/ppermute | solution.py:41
  94.4 0.9 reshape.67
  95.3 5.5 %all-to-all-start = ((bf16[8,81,128]{2,1,0:T(8,128)(2,1)}), bf16[8,81,128]{2,1,0:T(8,128)(2,1)S(1)}, u32[]{:S(2)}, u32[]{:S(2)}) async-start(bf16[8,81,128]{2,1,0:T(8,128)(2,1)} %reshape.67), calls=%async_computation | async-start | bytes 360448 | tf_op jit(solution)/shard_map/all_to_all | solution.py:456
  100.8 8.4 %all-to-all-done = bf16[8,81,128]{2,1,0:T(8,128)(2,1)S(1)} async-done(((bf16[8,81,128]{2,1,0:T(8,128)(2,1)}), bf16[8,81,128]{2,1,0:T(8,128)(2,1)S(1)}, u32[]{:S(2)}, u32[]{:S(2)}) %all-to-all-start) | async-done | bytes 165920 | tf_op jit(solution)/shard_map/all_to_all | solution.py:456
  109.3 5.5 %collective-permute-start.15 = (f32[81,128]{1,0:T(8,128)S(1)}, f32[81,128]{1,0:T(8,128)S(1)}, u32[]{:S(2)}, u32[]{:S(2)}) collective-permute-start(f32[81,128]{1,0:T(8,128)S(1)} %convert_reduce_fusion), channel_id=1, source_target_pairs={{0,1},{8,0},{32,33},{40,32},{64,65},{72,64},{96,97},{104,96},{128,... | collective-permute-start | bytes 124424 | tf_op jit(solution)/shard_map/ppermute | solution.py:41
  114.8 3.2 %collective-permute-start.16 = (f32[81,128]{1,0:T(8,128)S(1)}, f32[81,128]{1,0:T(8,128)S(1)}, u32[]{:S(2)}, u32[]{:S(2)}) collective-permute-start(f32[81,128]{1,0:T(8,128)S(1)} %convert_reduce_fusion), channel_id=1, source_target_pairs={{8,1},{40,33},{72,65},{104,97},{136,129},{168,161},{200,193},{232,... | collective-permute-start | bytes 124424 | tf_op jit(solution)/shard_map/ppermute | solution.py:41
  118.1 3.6 %collective-permute-done.16 = f32[81,128]{1,0:T(8,128)S(1)} collective-permute-done((f32[81,128]{1,0:T(8,128)S(1)}, f32[81,128]{1,0:T(8,128)S(1)}, u32[]{:S(2)}, u32[]{:S(2)}) %collective-permute-start.16) | collective-permute-done | bytes 41504 | tf_op jit(solution)/shard_map/ppermute | solution.py:41
  122.0 1.5 %collective-permute-start.18 = (f32[2,81,128]{2,0,1:T(2,128)S(1)}, f32[2,81,128]{2,0,1:T(2,128)S(1)}, u32[]{:S(2)}, u32[]{:S(2)}) collective-permute-start(f32[2,81,128]{2,0,1:T(2,128)S(1)} %get-tuple-element.54), channel_id=1, source_target_pairs={{0,4},{8,12},{32,36},{40,44},{64,68},{72,76},{96,100},{104,108},{1... | collective-permute-start | bytes 248840 | tf_op jit(solution)/shard_map/ppermute | solution.py:41
  123.5 1.2 collective-permute-start.19
  124.6 2.7 %collective-permute-done.17 = f32[2,81,128]{2,0,1:T(2,128)S(1)} collective-permute-done((f32[2,81,128]{2,0,1:T(2,128)S(1)}, f32[2,81,128]{2,0,1:T(2,128)S(1)}, u32[]{:S(2)}, u32[]{:S(2)}) %collective-permute-start.17) | collective-permute-done | bytes 82976 | tf_op jit(solution)/shard_map/ppermute | solution.py:41
  128.1 0.9 gather_fusion
  129.2 0.9 slice_reduce_fusion
  (57 shorter events, 11.9 us)
Async XLA Ops:
  0.6 19.5 %collective-permute-start.4 = (bf16[224,1152]{1,0:T(8,128)(2,1)}, bf16[224,1152]{1,0:T(8,128)(2,1)S(1)}, u32[]{:S(2)}, u32[]{:S(2)}) collective-permute-start(bf16[224,1152]{1,0:T(8,128)(2,1)} %im.1), channel_id=1, source_target_pairs={{0,8},{8,0},{32,40},{40,32},{64,72},{72,64},{96,104},{104,96},{128... | collective-permute-start | bytes 1548296 | tf_op jit(solution)/shard_map/ppermute | solution.py:41
  4.0 16.2 %collective-permute-start.5 = (bf16[224,1152]{1,0:T(8,128)(2,1)}, bf16[224,1152]{1,0:T(8,128)(2,1)S(1)}, u32[]{:S(2)}, u32[]{:S(2)}) collective-permute-start(bf16[224,1152]{1,0:T(8,128)(2,1)} %cm.1), channel_id=1, source_target_pairs={{0,8},{8,0},{32,40},{40,32},{64,72},{72,64},{96,104},{104,96},{128... | collective-permute-start | bytes 1548296 | tf_op jit(solution)/shard_map/ppermute | solution.py:41
  4.7 29.0 %collective-permute-start.1 = (bf16[224,1152]{1,0:T(8,128)(2,1)}, bf16[224,1152]{1,0:T(8,128)(2,1)S(1)}, u32[]{:S(2)}, u32[]{:S(2)}) collective-permute-start(bf16[224,1152]{1,0:T(8,128)(2,1)} %im.1), channel_id=1, source_target_pairs={{0,224},{8,232},{32,0},{40,8},{64,32},{72,40},{96,64},{104,72},{12... | collective-permute-start | bytes 1548296 | tf_op jit(solution)/shard_map/ppermute | solution.py:41
  8.6 25.1 %collective-permute-start.2 = (bf16[224,1152]{1,0:T(8,128)(2,1)}, bf16[224,1152]{1,0:T(8,128)(2,1)S(1)}, u32[]{:S(2)}, u32[]{:S(2)}) collective-permute-start(bf16[224,1152]{1,0:T(8,128)(2,1)} %im.1), channel_id=1, source_target_pairs={{16,240},{48,16},{80,48},{112,80},{144,112},{176,144},{208,176},{2... | collective-permute-start | bytes 1548296 | tf_op jit(solution)/shard_map/ppermute | solution.py:41
  9.3 6.8 %collective-permute-start.3 = (s32[224]{0:T(256)}, s32[224]{0:T(256)S(1)}, u32[]{:S(2)}, u32[]{:S(2)}) collective-permute-start(s32[224]{0:T(256)} %param.16), channel_id=1, source_target_pairs={{0,8},{8,0},{32,40},{40,32},{64,72},{72,64},{96,104},{104,96},{128... | collective-permute-start | bytes 2696 | tf_op jit(solution)/shard_map/ppermute | solution.py:41
  10.9 2.6 %copy-start = (s32[224]{0:T(256)S(1)}, s32[224]{0:T(256)}, u32[]{:S(2)}) copy-start(s32[224]{0:T(256)} %param.16) | copy-start | bytes 2692
  10.9 5.3 %copy-start.1 = (bf16[224,1152]{1,0:T(8,128)(2,1)S(1)}, bf16[224,1152]{1,0:T(8,128)(2,1)}, u32[]{:S(2)}) copy-start(bf16[224,1152]{1,0:T(8,128)(2,1)} %cm.1) | copy-start | bytes 1548292
  16.2 17.5 %collective-permute-start = (bf16[224,1152]{1,0:T(8,128)(2,1)S(1)}, bf16[224,1152]{1,0:T(8,128)(2,1)S(1)}, u32[]{:S(2)}, u32[]{:S(2)}) collective-permute-start(bf16[224,1152]{1,0:T(8,128)(2,1)S(1)} %copy-done.1), channel_id=1, source_target_pairs={{0,16},{8,24},{32,48},{40,56},{64,80},{72,88},{96,112},{104,120},{... | collective-permute-start | bytes 1548296 | tf_op jit(solution)/shard_map/ppermute | solution.py:41
  20.1 0.8 copy-start.4
  20.1 1.0 copy-start.5
  33.7 3.5 %copy-start.2 = (bf16[224,1152]{1,0:T(8,128)(2,1)}, bf16[224,1152]{1,0:T(8,128)(2,1)S(1)}, u32[]{:S(2)}) copy-start(bf16[224,1152]{1,0:T(8,128)(2,1)S(1)} %collective-permute-done.1.fm) | copy-start | bytes 1548292
  33.7 3.5 %copy-start.3 = (bf16[224,1152]{1,0:T(8,128)(2,1)}, bf16[224,1152]{1,0:T(8,128)(2,1)S(1)}, u32[]{:S(2)}) copy-start(bf16[224,1152]{1,0:T(8,128)(2,1)S(1)} %collective-permute-done.2.em) | copy-start | bytes 1548292
  33.7 3.5 %copy-start.6 = (bf16[224,1152]{1,0:T(8,128)(2,1)}, bf16[224,1152]{1,0:T(8,128)(2,1)S(1)}, u32[]{:S(2)}) copy-start(bf16[224,1152]{1,0:T(8,128)(2,1)S(1)} %collective-permute-done.sm) | copy-start | bytes 1548292
  33.7 2.0 %collective-permute-start.6 = (bf16[224,1152]{1,0:T(8,128)(2,1)S(1)}, bf16[224,1152]{1,0:T(8,128)(2,1)S(1)}, u32[]{:S(2)}, u32[]{:S(2)}) collective-permute-start(bf16[224,1152]{1,0:T(8,128)(2,1)S(1)} %collective-permute-done.sm), channel_id=1, source_target_pairs={{0,8},{8,0},{32,40},{40,32},{64,72},{72,64},{96,104},{104,96},{128... | collective-permute-start | bytes 1548296 | tf_op jit(solution)/shard_map/ppermute | solution.py:41
  34.1 2.3 %collective-permute-start.7 = (bf16[224,1152]{1,0:T(8,128)(2,1)S(1)}, bf16[224,1152]{1,0:T(8,128)(2,1)S(1)}, u32[]{:S(2)}, u32[]{:S(2)}) collective-permute-start(bf16[224,1152]{1,0:T(8,128)(2,1)S(1)} %collective-permute-done.1.fm), channel_id=1, source_target_pairs={{0,8},{8,0},{32,40},{40,32},{64,72},{72,64},{96,104},{104,96},{128... | collective-permute-start | bytes 1548296 | tf_op jit(solution)/shard_map/ppermute | solution.py:41
  34.3 2.9 %collective-permute-start.8 = (bf16[224,1152]{1,0:T(8,128)(2,1)S(1)}, bf16[224,1152]{1,0:T(8,128)(2,1)S(1)}, u32[]{:S(2)}, u32[]{:S(2)}) collective-permute-start(bf16[224,1152]{1,0:T(8,128)(2,1)S(1)} %collective-permute-done.2.em), channel_id=1, source_target_pairs={{0,8},{8,0},{32,40},{40,32},{64,72},{72,64},{96,104},{104,96},{128... | collective-permute-start | bytes 1548296 | tf_op jit(solution)/shard_map/ppermute | solution.py:41
  35.7 1.5 %copy-start.7 = (bf16[224,1152]{1,0:T(8,128)(2,1)}, bf16[224,1152]{1,0:T(8,128)(2,1)S(1)}, u32[]{:S(2)}) copy-start(bf16[224,1152]{1,0:T(8,128)(2,1)S(1)} %collective-permute-done.6.so) | copy-start | bytes 1548292
  36.4 0.8 copy-start.8
  37.2 0.8 copy-start.9
  64.2 10.1 %collective-permute-start.10 = (bf16[288,1152]{1,0:T(8,128)(2,1)}, bf16[288,1152]{1,0:T(8,128)(2,1)S(1)}, u32[]{:S(2)}, u32[]{:S(2)}) collective-permute-start(bf16[288,1152]{1,0:T(8,128)(2,1)} %get-tuple-element.44), channel_id=1, source_target_pairs={{0,6},{8,25},{32,38},{40,57},{64,70},{72,89},{96,102},{104,121},{1... | collective-permute-start | bytes 1990664 | tf_op jit(solution)/shard_map/ppermute | solution.py:41
  65.7 11.6 %collective-permute-start.11 = (bf16[288,1152]{1,0:T(8,128)(2,1)}, bf16[288,1152]{1,0:T(8,128)(2,1)S(1)}, u32[]{:S(2)}, u32[]{:S(2)}) collective-permute-start(bf16[288,1152]{1,0:T(8,128)(2,1)} %get-tuple-element.45), channel_id=1, source_target_pairs={{0,4},{8,9},{32,36},{40,41},{64,68},{72,73},{96,100},{104,105},{12... | collective-permute-start | bytes 1990664 | tf_op jit(solution)/shard_map/ppermute | solution.py:41
  67.0 17.4 %collective-permute-start.9 = (bf16[288,1152]{1,0:T(8,128)(2,1)}, bf16[288,1152]{1,0:T(8,128)(2,1)S(1)}, u32[]{:S(2)}, u32[]{:S(2)}) collective-permute-start(bf16[288,1152]{1,0:T(8,128)(2,1)} %get-tuple-element.43), channel_id=1, source_target_pairs={{0,2},{8,24},{32,34},{40,56},{64,66},{72,88},{96,98},{104,120},{12... | collective-permute-start | bytes 1990664 | tf_op jit(solution)/shard_map/ppermute | solution.py:41
  85.8 5.5 %collective-permute-start.12 = (bf16[72,1152]{1,0:T(8,128)(2,1)S(1)}, bf16[72,1152]{1,0:T(8,128)(2,1)S(1)}, u32[]{:S(2)}, u32[]{:S(2)}) collective-permute-start(bf16[72,1152]{1,0:T(8,128)(2,1)S(1)} %get-tuple-element.48), channel_id=1, source_target_pairs={{0,16},{8,10},{32,48},{40,42},{64,80},{72,74},{96,112},{104,106},{... | collective-permute-start | bytes 497672 | tf_op jit(solution)/shard_map/ppermute | solution.py:41
  86.8 5.8 %collective-permute-start.13 = (bf16[72,1152]{1,0:T(8,128)(2,1)S(1)}, bf16[72,1152]{1,0:T(8,128)(2,1)S(1)}, u32[]{:S(2)}, u32[]{:S(2)}) collective-permute-start(bf16[72,1152]{1,0:T(8,128)(2,1)S(1)} %get-tuple-element.50), channel_id=1, source_target_pairs={{0,17},{8,14},{32,49},{40,46},{64,81},{72,78},{96,113},{104,110},{... | collective-permute-start | bytes 497672 | tf_op jit(solution)/shard_map/ppermute | solution.py:41
  88.6 5.7 %collective-permute-start.14 = (bf16[72,1152]{1,0:T(8,128)(2,1)S(1)}, bf16[72,1152]{1,0:T(8,128)(2,1)S(1)}, u32[]{:S(2)}, u32[]{:S(2)}) collective-permute-start(bf16[72,1152]{1,0:T(8,128)(2,1)S(1)} %get-tuple-element.49), channel_id=1, source_target_pairs={{0,1},{8,12},{32,33},{40,44},{64,65},{72,76},{96,97},{104,108},{12... | collective-permute-start | bytes 497672 | tf_op jit(solution)/shard_map/ppermute | solution.py:41
  95.3 14.0 %all-to-all-start = ((bf16[8,81,128]{2,1,0:T(8,128)(2,1)}), bf16[8,81,128]{2,1,0:T(8,128)(2,1)S(1)}, u32[]{:S(2)}, u32[]{:S(2)}) async-start(bf16[8,81,128]{2,1,0:T(8,128)(2,1)} %reshape.67), calls=%async_computation | async-start | bytes 360448 | tf_op jit(solution)/shard_map/all_to_all | solution.py:456
  109.3 8.8 %collective-permute-start.15 = (f32[81,128]{1,0:T(8,128)S(1)}, f32[81,128]{1,0:T(8,128)S(1)}, u32[]{:S(2)}, u32[]{:S(2)}) collective-permute-start(f32[81,128]{1,0:T(8,128)S(1)} %convert_reduce_fusion), channel_id=1, source_target_pairs={{0,1},{8,0},{32,33},{40,32},{64,65},{72,64},{96,97},{104,96},{128,... | collective-permute-start | bytes 124424 | tf_op jit(solution)/shard_map/ppermute | solution.py:41
  114.8 6.9 %collective-permute-start.16 = (f32[81,128]{1,0:T(8,128)S(1)}, f32[81,128]{1,0:T(8,128)S(1)}, u32[]{:S(2)}, u32[]{:S(2)}) collective-permute-start(f32[81,128]{1,0:T(8,128)S(1)} %convert_reduce_fusion), channel_id=1, source_target_pairs={{8,1},{40,33},{72,65},{104,97},{136,129},{168,161},{200,193},{232,... | collective-permute-start | bytes 124424 | tf_op jit(solution)/shard_map/ppermute | solution.py:41
  121.9 5.5 %collective-permute-start.17 = (f32[2,81,128]{2,0,1:T(2,128)S(1)}, f32[2,81,128]{2,0,1:T(2,128)S(1)}, u32[]{:S(2)}, u32[]{:S(2)}) collective-permute-start(f32[2,81,128]{2,0,1:T(2,128)S(1)} %get-tuple-element.54), channel_id=1, source_target_pairs={{0,2},{8,10},{32,34},{40,42},{64,66},{72,74},{96,98},{104,106},{12... | collective-permute-start | bytes 248840 | tf_op jit(solution)/shard_map/ppermute | solution.py:41
  122.0 5.4 %collective-permute-start.18 = (f32[2,81,128]{2,0,1:T(2,128)S(1)}, f32[2,81,128]{2,0,1:T(2,128)S(1)}, u32[]{:S(2)}, u32[]{:S(2)}) collective-permute-start(f32[2,81,128]{2,0,1:T(2,128)S(1)} %get-tuple-element.54), channel_id=1, source_target_pairs={{0,4},{8,12},{32,36},{40,44},{64,68},{72,76},{96,100},{104,108},{1... | collective-permute-start | bytes 248840 | tf_op jit(solution)/shard_map/ppermute | solution.py:41
  123.5 4.5 %collective-permute-start.19 = (f32[2,81,128]{2,0,1:T(2,128)S(1)}, f32[2,81,128]{2,0,1:T(2,128)S(1)}, u32[]{:S(2)}, u32[]{:S(2)}) collective-permute-start(f32[2,81,128]{2,0,1:T(2,128)S(1)} %get-tuple-element.54), channel_id=1, source_target_pairs={{0,6},{8,14},{32,38},{40,46},{64,70},{72,78},{96,102},{104,110},{1... | collective-permute-start | bytes 248840 | tf_op jit(solution)/shard_map/ppermute | solution.py:41

commit v2 on v1

--- a/solution.py
+++ b/solution.py
@@ -23,15 +23,6 @@
 ALONG_Z = [[device_at(x, y, z, c) for z in range(NZ)] for x in range(NX) for y in range(NY) for c in range(2)]
 
 
-def row_order(core, x, y):
-    rows = np.arange(D)
-    ninth, z = rows % 9, rows // 9 % 8
-    one, two = rows // 288, rows // 72 % 4
-    to_x = (x + jnp.where(core == 0, one, two)) % NX
-    to_y = (y + jnp.where(core == 0, two, one)) % NY
-    return (z * 2 + to_y % 2) * 72 + to_y // 2 * 36 + to_x * 9 + ninth
-
-
 def moved(value, to):
     pairs = []
     for place in PLACES:
@@ -91,6 +82,12 @@
 TAKEN = ((APART >= -3) & (APART <= 2)).astype(float).tolist()
 
 
+def row_code():
+    rows = np.arange(D)
+    base = rows // 9 % 8 * 144 + rows % 9
+    return (base + (rows // 288 << 12) + (rows // 72 % 4 << 14)).astype(np.int32)[:, None]
+
+
 def nt_dot(a, b):
     return lax.dot_general(a, b, (((1,), (1,)), ((), ())), preferred_element_type=F32)
 
@@ -124,6 +121,17 @@
         tmp[0:rows, n : n + w] = p
         squares = squares + jnp.sum(p * p, axis=1, keepdims=True)
     return lax.rsqrt(squares + 1e-6)
+
+
+def one_hot(place_ref, code_ref, pv):
+    core, x, y = place_ref[0], place_ref[2], place_ref[3]
+    for n, w in THIRDS:
+        code = code_ref[n : n + w]
+        one, two = (code >> 12) & 3, (code >> 14) & 3
+        to_x = (x + jnp.where(core == 0, one, two)) & 3
+        to_y = (y + jnp.where(core == 0, two, one)) & 3
+        order = (code & 4095) + (to_y & 1) * 72 + (to_y >> 1) * 36 + to_x * 9
+        pv[n : n + w] = jnp.where(lax.broadcasted_iota(jnp.int32, (w, D), 1) == order, 1.0, 0.0).astype(BF16)
 
 
 def pair_weights(scalars, rows, cols, xs, height, ys, scale_of, gs, label=None):
@@ -142,9 +150,9 @@
 
 
 def own_kernel(
-    place_ref, sharp_ref, shift_ref, coef_ref, mine_c, other_c, mine_r, other_r, im, io, cm, co, wi, wc, order,
-    zx_out, zy_out, ux_out, ix_out, ft_out, dz_out,
-    f, w, pv, tmp, zx, zy, ux, ix, gs, ft, dz, sems,
+    place_ref, sharp_ref, shift_ref, coef_ref, code_ref, mine_ref, other_ref, im, io, cm, co, wi, wc,
+    pv_out, zx_out, zy_out, ux_out, ix_out, ft_out, dz_out,
+    f, w, pv, tmp, zx, zy, ux, ix, gs, ft, dz, targets, sems,
 ):
     core = place_ref[0]
     first = by_role(
@@ -155,6 +163,11 @@
         place_ref, [(cm, io, f.at[1, pl.ds(0, R)]), (co, im, f.at[1, pl.ds(R, R)]), (wc, wi, w.at[1])],
         sems.at[pl.ds(3, 3)],
     )
+    one_hot(place_ref, code_ref, pv)
+    outs = [fetch(pv, pv_out, sems.at[9])]
+    targets[...] = jnp.full((2, PAD), -1, jnp.int32)
+    targets[0:1, 0:R] = jnp.where(core == 0, mine_ref[...], other_ref[...])
+    targets[1:2, 0:R] = jnp.where(core == 0, other_ref[...], mine_ref[...])
     for wait in first:
         wait.wait()
     inv = project(f[0], w.at[0], tmp, 2 * R)
@@ -162,10 +175,9 @@
     unit = tmp[...] * inv
     ux[...] = unit
     zx[...] = unit.astype(BF16)
-    outs = [fetch(ux, ux_out, sems.at[6]), fetch(zx, zx_out, sems.at[7]), fetch(ix, ix_out, sems.at[8])]
+    outs += [fetch(ux, ux_out, sems.at[6]), fetch(zx, zx_out, sems.at[7]), fetch(ix, ix_out, sems.at[8])]
     for wait in second:
         wait.wait()
-    late = fetch(order, pv, sems.at[9])
     inv = project(f[1], w.at[1], tmp, 2 * R)
     for b in range(2):
         zy[b * PAD : b * PAD + R] = (tmp[b * R : (b + 1) * R] * inv[b * R : (b + 1) * R]).astype(BF16)
@@ -173,15 +185,11 @@
     outs.append(fetch(zy, zy_out, sems.at[10]))
 
     def label(k):
-        mine = core == k
-        by_col = jnp.where(mine, mine_c[...], other_c[...])
-        by_row = jnp.where(mine, mine_r[...], other_r[...])
-        shape = (R, PAD)
-        target = jnp.where(core == 0, jnp.broadcast_to(by_col, shape), jnp.broadcast_to(by_row, shape))
-        place = jnp.where(
-            core == 0, lax.broadcasted_iota(jnp.int32, shape, 1), lax.broadcasted_iota(jnp.int32, shape, 0)
-        )
-        return place == target
+        down, across = lax.broadcasted_iota(jnp.int32, (R, PAD), 0), lax.broadcasted_iota(jnp.int32, (R, PAD), 1)
+        by_row = jnp.broadcast_to(targets[k : k + 1], (R, PAD))
+        by_col = jnp.sum(jnp.where(down == across, by_row, 0), axis=1, keepdims=True)
+        target = jnp.where(core == 0, jnp.broadcast_to(by_col, (R, PAD)), by_row)
+        return jnp.where(core == 0, across, down) == target
 
     scalars = (sharp_ref[0], shift_ref[0])
     pair_weights(scalars, zx[...], zy[...], (0, 1), R, (0, 1), lambda x, y: coef_ref[0], gs, label)
@@ -192,7 +200,6 @@
         dz[:, cols] = sharp_ref[0] * jnp.dot(gs[...], zy[:, cols], preferred_element_type=F32)
 
     outs.append(fetch(dz, dz_out, sems.at[11]))
-    late.wait()
 
     @pl.loop(0, 3)
     def _(k):
@@ -204,19 +211,19 @@
         copy.wait()
 
 
-def own_part(place, sharp, shift, coef, mine_c, other_c, mine_r, other_r, *operands):
+def own_part(place, sharp, shift, coef, code, mine, other, *operands):
     smem = pl.BlockSpec(memory_space=pltpu.SMEM)
     vmem = pl.BlockSpec(memory_space=pltpu.VMEM)
     hbm = pl.BlockSpec(memory_space=pl.ANY)
     results = [
-        ((2 * R, D), BF16), ((2 * PAD, D), BF16), ((2 * R, D), F32), ((2 * R, 128), F32), ((D, 2 * PAD), BF16),
+        ((D, D), BF16), ((2 * R, D), BF16), ((2 * PAD, D), BF16), ((2 * R, D), F32), ((2 * R, 128), F32), ((D, 2 * PAD), BF16),
         ((2 * R, D), F32),
     ]
     return pl.pallas_call(
         own_kernel,
         out_shape=[jax.ShapeDtypeStruct(*result) for result in results],
-        in_specs=[smem] * 4 + [vmem] * 4 + [hbm] * 7,
-        out_specs=[hbm] * 6,
+        in_specs=[smem] * 4 + [vmem] * 3 + [hbm] * 6,
+        out_specs=[hbm] * 7,
         scratch_shapes=[
             pltpu.VMEM((2, 2 * R, D), BF16),
             pltpu.VMEM((2, D, D), BF16),
@@ -229,11 +236,12 @@
             pltpu.VMEM((2 * R, 2 * PAD), BF16),
             pltpu.VMEM((D, 2 * PAD), BF16),
             pltpu.VMEM((2 * R, D), F32),
+            pltpu.VMEM((2, PAD), jnp.int32),
             pltpu.SemaphoreType.DMA((13,)),
         ],
-        compiler_params=pltpu.CompilerParams(vmem_limit_bytes=60 * 2**20),
+        compiler_params=pltpu.CompilerParams(vmem_limit_bytes=30 * 2**20),
         cost_estimate=pl.CostEstimate(flops=6 * 10**9, bytes_accessed=16 * 10**6, transcendentals=500000),
-    )(place, sharp, shift, coef, mine_c, other_c, mine_r, other_r, *operands)
+    )(place, sharp, shift, coef, code, mine, other, *operands)
 
 
 def arrived_kernel(
@@ -395,9 +403,32 @@
             pltpu.VMEM((R, D), F32),
             pltpu.SemaphoreType.DMA((14,)),
         ],
-        compiler_params=pltpu.CompilerParams(vmem_limit_bytes=60 * 2**20),
+        compiler_params=pltpu.CompilerParams(vmem_limit_bytes=46 * 2**20),
         cost_estimate=pl.CostEstimate(flops=14 * 10**9, bytes_accessed=20 * 10**6, transcendentals=800000),
     )(place, sharp, shift, coef, *operands)
+
+
+def join_kernel(place_ref, one, two, three, four, image_out, caption_out, held):
+    for k, piece in enumerate((one, two, three, four)):
+        held[k] = piece[...]
+    for place in range(NX):
+        back = (place_ref[2] - place) & 3
+        for head, out in enumerate((image_out, caption_out)):
+            for row in range(9):
+                at = place * 9 + row
+                for n in range(9):
+                    out[at : at + 1, n * 128 : (n + 1) * 128] = held[back, head, row * 9 + n : row * 9 + n + 1]
+
+
+def join_rows(place, *pieces):
+    vmem = pl.BlockSpec(memory_space=pltpu.VMEM)
+    return pl.pallas_call(
+        join_kernel,
+        out_shape=[jax.ShapeDtypeStruct((36, D), F32)] * 2,
+        in_specs=[pl.BlockSpec(memory_space=pltpu.SMEM)] + [vmem] * 4,
+        out_specs=[vmem] * 2,
+        scratch_shapes=[pltpu.VMEM((4, 2, 81, 128), F32)],
+    )(place, *pieces)
 
 
 def local(
@@ -420,32 +451,29 @@
     own_img = swap_cores(picture_encoder_features)
     own_cap = swap_cores(text_encoder_features)
     target_other = swap_cores(matching_target)
-    cap, img, coefficient = lax.optimization_barrier(
-        (text_encoder_features, picture_encoder_features, coefficient)
+    cap, img, target_other = lax.optimization_barrier(
+        (text_encoder_features, picture_encoder_features, target_other)
     )
     cap_sib = swap_chips(cap)
     img_far = image_to_neighbour(img)
     img_extra = image_down(img)
 
-    def wide(target):
-        return jnp.pad(target, (0, PAD - R), constant_values=-1)[None]
-
-    order = row_order(core, x, y).astype(jnp.int32)
-    one_hot = (lax.broadcasted_iota(jnp.int32, (D, D), 1) == order[:, None]).astype(BF16)
-    kept = own_part(
-        role, sharpness_param, offset_shift, coefficient,
-        matching_target[:, None], target_other[:, None], wide(matching_target), wide(target_other),
+    order, *kept = own_part(
+        role, sharpness_param, offset_shift, coefficient, row_code(),
+        matching_target[None], target_other[None],
         picture_encoder_features, own_img, text_encoder_features, own_cap,
-        picture_projector, text_projector, one_hot,
-    )
-    cap_sib, img_far, img_extra, kept = lax.optimization_barrier((cap_sib, img_far, img_extra, kept))
+        picture_projector, text_projector,
+    )
+    cap_sib, img_far, img_extra, order, kept = lax.optimization_barrier(
+        (cap_sib, img_far, img_extra, order, kept)
+    )
     cap_sib_other = swap_cores(cap_sib)
     img_far_other = swap_cores(img_far)
     img_extra_other = swap_cores(img_extra)
     parts = arrived_part(
         role, sharpness_param, offset_shift, coefficient,
         cap_sib, cap_sib_other, img_far, img_far_other, img_extra, img_extra_other,
-        picture_projector, text_projector, one_hot, *kept,
+        picture_projector, text_projector, order, *kept,
     )
 
     one = [parts[0]] + [first_axis(parts[by], by) for by in (1, 3, 2)]
@@ -462,9 +490,7 @@
     image_piece = jnp.where(home & first, mine, jnp.where(home | first, ring, cross))
     caption_piece = jnp.where(home & first, ring, jnp.where(home, mine, jnp.where(first, cross, ring)))
     both = jnp.stack([image_piece, caption_piece])
-    held = jnp.stack([both] + [along_x(both, by) for by in (1, 2, 3)])
-    rows = jnp.take(held, (x - jnp.arange(NX)) % NX, axis=0).transpose(1, 0, 2, 3).reshape(2, 36, D)
-    return (rows[0], rows[1])
+    return join_rows(role, both, *[along_x(both, by) for by in (1, 2, 3)])
 
 
 def solution(mesh):

time: 132 us -> 134 us (1.015)
  blocking collectives: 0 us -> 13.8 us
  waiting for transfers between devices: 38.9 us -> 30.2 us
  starting transfers between devices: 36.9 us -> 31.6 us
  other arithmetic: 5.42 us -> 0.57 us
  local copies, waits for them, and re-layouts: 8.76 us -> 13.5 us
  Pallas kernels: 38.7 us -> 41.5 us
    all_to_all x0 -> x1, blocking collectives: none -> 13.8 us  [local(): three = lax.all_to_all(two, AXES, 0, 0, axis_index_groups=ALONG_Z)]
    unnamed x20 -> x30, local copies, waits for them, and re-layouts: 1.86 us -> 13.3 us
    all_to_all x1 -> x0, waiting for transfers between devices: 8.44 us -> none  [local(): three = lax.all_to_all(two, AXES, 0, 0, axis_index_groups=ALONG_Z)]
    all_to_all x1 -> x0, starting transfers between devices: 5.54 us -> none  [local(): three = lax.all_to_all(two, AXES, 0, 0, axis_index_groups=ALONG_Z)]
    convert_element_type x1 -> x0, other arithmetic: 2.03 us -> none  [local(): (lax.broadcasted_iota(jnp.int32, (D, D), 1) == order[:, None]).astype(BF16)]
    pallas_call x0 -> x1, Pallas kernels: none -> 2.01 us  [join_rows(): pl.pallas_call(join_kernel, out_shape=[jax.ShapeDtypeStruct((36, D), F32)...]
    broadcast_in_dim x2 -> x0, local copies, waits for them, and re-layouts: 1.56 us -> none  [the longest x1 0.78 us: local(): matching_target[:, None]]
    pallas_call x1, Pallas kernels: 12.6 us -> 14.1 us  [own_part(): pl.pallas_call(own_kernel, out_shape=[jax.ShapeDtypeStruct(*result) for r...]
  transfers between devices with their start and end apart: 21 -> 20, of which waited for: 13 -> 12; matrix products, arithmetic and copies ran while one was open for 5% -> 0% of each run, Pallas kernels for 10% -> 11%
where the time goes in v2:
time: 134 us
  Pallas kernels  41.5 us (31%)
  starting transfers between devices  31.6 us (24%)
  waiting for transfers between devices  30.2 us (23%)
  blocking collectives  13.8 us (10%)
  local copies, waits for them, and re-layouts  13.5 us (10%)
  between operations  2.76 us (2%)
    ppermute x20, starting transfers between devices, moved(): return lax.ppermute(value, AXES, pairs)  31.6 us
    ppermute x20, waiting for transfers between devices, moved(): return lax.ppermute(value, AXES, pairs)  30.2 us
    pallas_call x1, Pallas kernels, arrived_part(): pl.pallas_call(arrived_kernel, out_shape=[jax.ShapeDtypeStruct((D // 4, D...  25.4 us
    pallas_call x1, Pallas kernels, own_part(): pl.pallas_call(own_kernel, out_shape=[jax.ShapeDtypeStruct(*result) for r...  14.1 us
    all_to_all x1, blocking collectives, local(): three = lax.all_to_all(two, AXES, 0, 0, axis_index_groups=ALONG_Z)  13.8 us
    unnamed x30, local copies, waits for them, and re-layouts  13.3 us
  transfers between devices with their start and end apart: 20, of which 12 were waited for; matrix products, arithmetic and copies ran while one was open for 0% of the time, Pallas kernels for 11%

profile of v2, /device:TPU:1, one launch (start us, length us, event | category | flops | bytes accessed | tf_op | source)
XLA Modules:
  0.0 134.0 jit_solution(972822920111001547)
XLA Ops:
  0.6 3.3 %collective-permute-start.4 = (bf16[224,1152]{1,0:T(8,128)(2,1)}, bf16[224,1152]{1,0:T(8,128)(2,1)S(1)}, u32[]{:S(2)}, u32[]{:S(2)}) collective-permute-start(bf16[224,1152]{1,0:T(8,128)(2,1)} %im.1), channel_id=1, source_target_pairs={{0,8},{8,0},{32,40},{40,32},{64,72},{72,64},{96,104},{104,96},{128... | collective-permute-start | bytes 1548296 | tf_op jit(solution)/shard_map/ppermute | solution.py:32
  6.5 3.9 %collective-permute-start.2 = (bf16[224,1152]{1,0:T(8,128)(2,1)}, bf16[224,1152]{1,0:T(8,128)(2,1)S(1)}, u32[]{:S(2)}, u32[]{:S(2)}) collective-permute-start(bf16[224,1152]{1,0:T(8,128)(2,1)} %im.1), channel_id=1, source_target_pairs={{0,224},{8,232},{32,0},{40,8},{64,32},{72,40},{96,64},{104,72},{12... | collective-permute-start | bytes 1548296 | tf_op jit(solution)/shard_map/ppermute | solution.py:32
  11.2 1.7 %copy-done.1 = bf16[1152,1152]{1,0:T(8,128)(2,1)S(1)} copy-done((bf16[1152,1152]{1,0:T(8,128)(2,1)S(1)}, bf16[1152,1152]{1,0:T(8,128)(2,1)}, u32[]{:S(2)}) %copy-start.1) | copy-done | bytes 2654232
  13.0 1.7 %copy-done.2 = bf16[1152,1152]{1,0:T(8,128)(2,1)S(1)} copy-done((bf16[1152,1152]{1,0:T(8,128)(2,1)S(1)}, bf16[1152,1152]{1,0:T(8,128)(2,1)}, u32[]{:S(2)}) %copy-start.2) | copy-done | bytes 2654232
  14.7 1.0 copy-done.3
  15.8 1.0 copy-done.4
  17.5 1.1 copy-done.6
  18.6 14.1 %shard_map.104 = (bf16[1152,1152]{1,0:T(8,128)(2,1)S(1)}, bf16[448,1152]{1,0:T(8,128)(2,1)S(1)}, bf16[512,1152]{1,0:T(8,128)(2,1)S(1)}, f32[448,1152]{1,0:T(8,12...) custom-call(s32[4]{0:T(128)S(1)} %pad_add_fusion.place_ref, ...), custom_call_target="tpu_custom_call" | custom-call | flops 6000000000 | bytes 16000000 | tf_op jit(solution)/shard_map/pallas_call | solution.py:222
  32.7 1.5 %copy-done.7 = bf16[1152,1152]{1,0:T(8,128)(2,1)} copy-done((bf16[1152,1152]{1,0:T(8,128)(2,1)}, bf16[1152,1152]{1,0:T(8,128)(2,1)S(1)}, u32[]{:S(2)}) %copy-start.7) | copy-done | bytes 2654232
  34.2 1.3 copy-done.8
  35.5 1.4 %copy-done.9 = f32[448,1152]{1,0:T(8,128)} copy-done((f32[448,1152]{1,0:T(8,128)}, f32[448,1152]{1,0:T(8,128)S(1)}, u32[]{:S(2)}) %copy-start.9) | copy-done | bytes 2064408
  36.8 1.1 copy-done.10
  37.9 3.4 %collective-permute-start.6 = (bf16[224,1152]{1,0:T(8,128)(2,1)S(1)}, bf16[224,1152]{1,0:T(8,128)(2,1)S(1)}, u32[]{:S(2)}, u32[]{:S(2)}) collective-permute-start(bf16[224,1152]{1,0:T(8,128)(2,1)S(1)} %collective-permute-done.1.sm), channel_id=1, source_target_pairs={{0,8},{8,0},{32,40},{40,32},{64,72},{72,64},{96,104},{104,96},{128... | collective-permute-start | bytes 1548296 | tf_op jit(solution)/shard_map/ppermute | solution.py:32
  44.3 25.4 %shard_map.105 = (bf16[288,1152]{1,0:T(8,128)(2,1)S(1)}, bf16[288,1152]{1,0:T(8,128)(2,1)S(1)}, bf16[288,1152]{1,0:T(8,128)(2,1)S(1)}, bf16[288,1152]{1,0:T(8,128)(2,1)S(1)}) custom-call(s32[4]{0:T(128)S(1)} %pad_add_fusion.place_ref, f32[1]{0:T(128)S(6)} %copy.11.sharp_ref, f32[1]{0:T(128)S(6)} %copy.12.shift_ref, f32[1]{0:T(128)S(6)} %div.24.coef_ref, ...), custom_call_target="tpu_custom_call" | custom-call | flops 14000000000 | bytes 20000000 | tf_op jit(solution)/shard_map/pallas_call | solution.py:382
  69.7 1.3 collective-permute-start.10
  71.0 1.7 %collective-permute-start.11 = (bf16[288,1152]{1,0:T(8,128)(2,1)S(1)}, bf16[288,1152]{1,0:T(8,128)(2,1)S(1)}, u32[]{:S(2)}, u32[]{:S(2)}) collective-permute-start(bf16[288,1152]{1,0:T(8,128)(2,1)S(1)} %get-tuple-element.49), channel_id=1, source_target_pairs={{0,4},{8,9},{32,36},{40,41},{64,68},{72,73},{96,100},{104,105},{12... | collective-permute-start | bytes 1990664 | tf_op jit(solution)/shard_map/ppermute | solution.py:32
  73.3 6.3 %collective-permute-done.10 = bf16[288,1152]{1,0:T(8,128)(2,1)S(1)} collective-permute-done((bf16[288,1152]{1,0:T(8,128)(2,1)S(1)}, bf16[288,1152]{1,0:T(8,128)(2,1)S(1)}, u32[]{:S(2)}, u32[]{:S(2)}) %collective-permute-start.10) | collective-permute-done | bytes 663584 | tf_op jit(solution)/shard_map/ppermute | solution.py:32
  79.6 2.8 %collective-permute-done.11 = bf16[288,1152]{1,0:T(8,128)(2,1)S(1)} collective-permute-done((bf16[288,1152]{1,0:T(8,128)(2,1)S(1)}, bf16[288,1152]{1,0:T(8,128)(2,1)S(1)}, u32[]{:S(2)}, u32[]{:S(2)}) %collective-permute-start.11) | collective-permute-done | bytes 663584 | tf_op jit(solution)/shard_map/ppermute | solution.py:32
  82.3 7.1 %collective-permute-done.9 = bf16[288,1152]{1,0:T(8,128)(2,1)S(1)} collective-permute-done((bf16[288,1152]{1,0:T(8,128)(2,1)S(1)}, bf16[288,1152]{1,0:T(8,128)(2,1)S(1)}, u32[]{:S(2)}, u32[]{:S(2)}) %collective-permute-start.9) | collective-permute-done | bytes 663584 | tf_op jit(solution)/shard_map/ppermute | solution.py:32
  90.8 1.8 %collective-permute-start.13 = (bf16[72,1152]{1,0:T(8,128)(2,1)S(1)}, bf16[72,1152]{1,0:T(8,128)(2,1)S(1)}, u32[]{:S(2)}, u32[]{:S(2)}) collective-permute-start(bf16[72,1152]{1,0:T(8,128)(2,1)S(1)} %get-tuple-element.52), channel_id=1, source_target_pairs={{0,17},{8,14},{32,49},{40,46},{64,81},{72,78},{96,113},{104,110},{... | collective-permute-start | bytes 497672 | tf_op jit(solution)/shard_map/ppermute | solution.py:32
  92.6 1.2 collective-permute-start.14
  93.8 1.5 %collective-permute-done.12 = bf16[72,1152]{1,0:T(8,128)(2,1)S(1)} collective-permute-done((bf16[72,1152]{1,0:T(8,128)(2,1)S(1)}, bf16[72,1152]{1,0:T(8,128)(2,1)S(1)}, u32[]{:S(2)}, u32[]{:S(2)}) %collective-permute-start.12) | collective-permute-done | bytes 165920 | tf_op jit(solution)/shard_map/ppermute | solution.py:32
  95.3 1.3 collective-permute-done.13
  96.6 1.6 %collective-permute-done.14 = bf16[72,1152]{1,0:T(8,128)(2,1)S(1)} collective-permute-done((bf16[72,1152]{1,0:T(8,128)(2,1)S(1)}, bf16[72,1152]{1,0:T(8,128)(2,1)S(1)}, u32[]{:S(2)}, u32[]{:S(2)}) %collective-permute-start.14) | collective-permute-done | bytes 165920 | tf_op jit(solution)/shard_map/ppermute | solution.py:32
  98.6 13.8 %all_to_all.5 = bf16[8,81,128]{2,1,0:T(8,128)(2,1)S(1)} all-to-all(bf16[8,81,128]{2,1,0:T(8,128)(2,1)S(1)} %reshape.7), channel_id=1, replica_groups={{0,32,64,96,128,160,192,224},{8,40,72,104,136,168,200,232},{16,48,80,11..., dimensions={0} | all-to-all | bytes 331776 | tf_op jit(solution)/shard_map/all_to_all | solution.py:484
  112.4 5.7 %collective-permute-start.15 = (f32[81,128]{1,0:T(8,128)S(1)}, f32[81,128]{1,0:T(8,128)S(1)}, u32[]{:S(2)}, u32[]{:S(2)}) collective-permute-start(f32[81,128]{1,0:T(8,128)S(1)} %convert_reduce_fusion), channel_id=1, source_target_pairs={{0,1},{8,0},{32,33},{40,32},{64,65},{72,64},{96,97},{104,96},{128,... | collective-permute-start | bytes 124424 | tf_op jit(solution)/shard_map/ppermute | solution.py:32
  118.1 3.2 %collective-permute-start.16 = (f32[81,128]{1,0:T(8,128)S(1)}, f32[81,128]{1,0:T(8,128)S(1)}, u32[]{:S(2)}, u32[]{:S(2)}) collective-permute-start(f32[81,128]{1,0:T(8,128)S(1)} %convert_reduce_fusion), channel_id=1, source_target_pairs={{8,1},{40,33},{72,65},{104,97},{136,129},{168,161},{200,193},{232,... | collective-permute-start | bytes 124424 | tf_op jit(solution)/shard_map/ppermute | solution.py:32
  121.4 3.6 %collective-permute-done.16 = f32[81,128]{1,0:T(8,128)S(1)} collective-permute-done((f32[81,128]{1,0:T(8,128)S(1)}, f32[81,128]{1,0:T(8,128)S(1)}, u32[]{:S(2)}, u32[]{:S(2)}) %collective-permute-start.16) | collective-permute-done | bytes 41504 | tf_op jit(solution)/shard_map/ppermute | solution.py:32
  125.1 1.5 %collective-permute-start.18 = (f32[2,81,128]{2,1,0:T(8,128)S(1)}, f32[2,81,128]{2,1,0:T(8,128)S(1)}, u32[]{:S(2)}, u32[]{:S(2)}) collective-permute-start(f32[2,81,128]{2,1,0:T(8,128)S(1)} %pad_maximum_fusion.one), channel_id=1, source_target_pairs={{0,4},{8,12},{32,36},{40,44},{64,68},{72,76},{96,100},{104,108},{1... | collective-permute-start | bytes 248840 | tf_op jit(solution)/shard_map/ppermute | solution.py:32
  126.6 1.2 collective-permute-start.19
  127.8 2.9 %collective-permute-done.17.two = f32[2,81,128]{2,1,0:T(8,128)S(1)} collective-permute-done((f32[2,81,128]{2,1,0:T(8,128)S(1)}, f32[2,81,128]{2,1,0:T(8,128)S(1)}, u32[]{:S(2)}, u32[]{:S(2)}) %collective-permute-start.17) | collective-permute-done | bytes 82976 | tf_op jit(solution)/shard_map/ppermute | solution.py:32
  132.0 2.0 %shard_map.106 = (f32[36,1152]{1,0:T(8,128)}, f32[36,1152]{1,0:T(8,128)}) custom-call(s32[4]{0:T(128)} %copy-done, f32[2,81,128]{2,1,0:T(8,128)} %copy-done.11, f32[2,81,128]{2,1,0:T(8,128)} %copy-done.12, f32[2,81,128]{2,1,0:T(8,128)} %copy-done.13, f32[2,81,128]{2,1,0:T(8,128)} %copy-done.14), custom_call_target="tpu_custom_call" | custom-call | tf_op jit(solution)/shard_map/pallas_call | solution.py:425
  (50 shorter events, 8.7 us)
Async XLA Ops:
  0.6 10.6 %collective-permute-start.4 = (bf16[224,1152]{1,0:T(8,128)(2,1)}, bf16[224,1152]{1,0:T(8,128)(2,1)S(1)}, u32[]{:S(2)}, u32[]{:S(2)}) collective-permute-start(bf16[224,1152]{1,0:T(8,128)(2,1)} %im.1), channel_id=1, source_target_pairs={{0,8},{8,0},{32,40},{40,32},{64,72},{72,64},{96,104},{104,96},{128... | collective-permute-start | bytes 1548296 | tf_op jit(solution)/shard_map/ppermute | solution.py:32
  4.0 7.3 %collective-permute-start.5 = (bf16[224,1152]{1,0:T(8,128)(2,1)}, bf16[224,1152]{1,0:T(8,128)(2,1)S(1)}, u32[]{:S(2)}, u32[]{:S(2)}) collective-permute-start(bf16[224,1152]{1,0:T(8,128)(2,1)} %cm.1), channel_id=1, source_target_pairs={{0,8},{8,0},{32,40},{40,32},{64,72},{72,64},{96,104},{104,96},{128... | collective-permute-start | bytes 1548296 | tf_op jit(solution)/shard_map/ppermute | solution.py:32
  4.1 2.4 %collective-permute-start = (s32[224]{0:T(256)}, s32[224]{0:T(256)S(1)}, u32[]{:S(2)}, u32[]{:S(2)}) collective-permute-start(s32[224]{0:T(256)} %param.13), channel_id=1, source_target_pairs={{0,8},{8,0},{32,40},{40,32},{64,72},{72,64},{96,104},{104,96},{128... | collective-permute-start | bytes 2696 | tf_op jit(solution)/shard_map/ppermute | solution.py:32
  4.5 39.7 %copy-start = (s32[4]{0:T(128)}, s32[4]{0:T(128)S(1)}, u32[]{:S(2)}) copy-start(s32[4]{0:T(128)S(1)} %pad_add_fusion.place_ref) | copy-start | bytes 52
  6.5 31.4 %collective-permute-start.2 = (bf16[224,1152]{1,0:T(8,128)(2,1)}, bf16[224,1152]{1,0:T(8,128)(2,1)S(1)}, u32[]{:S(2)}, u32[]{:S(2)}) collective-permute-start(bf16[224,1152]{1,0:T(8,128)(2,1)} %im.1), channel_id=1, source_target_pairs={{0,224},{8,232},{32,0},{40,8},{64,32},{72,40},{96,64},{104,72},{12... | collective-permute-start | bytes 1548296 | tf_op jit(solution)/shard_map/ppermute | solution.py:32
  10.4 27.5 %collective-permute-start.3 = (bf16[224,1152]{1,0:T(8,128)(2,1)}, bf16[224,1152]{1,0:T(8,128)(2,1)S(1)}, u32[]{:S(2)}, u32[]{:S(2)}) collective-permute-start(bf16[224,1152]{1,0:T(8,128)(2,1)} %im.1), channel_id=1, source_target_pairs={{16,240},{48,16},{80,48},{112,80},{144,112},{176,144},{208,176},{2... | collective-permute-start | bytes 1548296 | tf_op jit(solution)/shard_map/ppermute | solution.py:32
  11.1 26.8 %collective-permute-start.1 = (bf16[224,1152]{1,0:T(8,128)(2,1)}, bf16[224,1152]{1,0:T(8,128)(2,1)S(1)}, u32[]{:S(2)}, u32[]{:S(2)}) collective-permute-start(bf16[224,1152]{1,0:T(8,128)(2,1)} %cm.1), channel_id=1, source_target_pairs={{0,16},{8,24},{32,48},{40,56},{64,80},{72,88},{96,112},{104,120},{... | collective-permute-start | bytes 1548296 | tf_op jit(solution)/shard_map/ppermute | solution.py:32
  11.2 1.8 %copy-start.1 = (bf16[1152,1152]{1,0:T(8,128)(2,1)S(1)}, bf16[1152,1152]{1,0:T(8,128)(2,1)}, u32[]{:S(2)}) copy-start(bf16[1152,1152]{1,0:T(8,128)(2,1)} %wi.3) | copy-start | bytes 7962628
  13.0 1.7 %copy-start.2 = (bf16[1152,1152]{1,0:T(8,128)(2,1)S(1)}, bf16[1152,1152]{1,0:T(8,128)(2,1)}, u32[]{:S(2)}) copy-start(bf16[1152,1152]{1,0:T(8,128)(2,1)} %wc.3) | copy-start | bytes 7962628
  14.7 1.0 copy-start.3
  15.8 1.0 copy-start.4
  16.8 0.7 copy-start.5
  17.5 1.1 copy-start.6
  32.6 1.5 %copy-start.7 = (bf16[1152,1152]{1,0:T(8,128)(2,1)}, bf16[1152,1152]{1,0:T(8,128)(2,1)S(1)}, u32[]{:S(2)}) copy-start(bf16[1152,1152]{1,0:T(8,128)(2,1)S(1)} %get-tuple-element.39.order) | copy-start | bytes 7962628
  34.2 1.3 copy-start.8
  35.5 1.4 %copy-start.9 = (f32[448,1152]{1,0:T(8,128)}, f32[448,1152]{1,0:T(8,128)S(1)}, u32[]{:S(2)}) copy-start(f32[448,1152]{1,0:T(8,128)S(1)} %get-tuple-element.45.dz_in) | copy-start | bytes 6193156
  36.8 1.1 copy-start.10
  37.9 4.9 %collective-permute-start.6 = (bf16[224,1152]{1,0:T(8,128)(2,1)S(1)}, bf16[224,1152]{1,0:T(8,128)(2,1)S(1)}, u32[]{:S(2)}, u32[]{:S(2)}) collective-permute-start(bf16[224,1152]{1,0:T(8,128)(2,1)S(1)} %collective-permute-done.1.sm), channel_id=1, source_target_pairs={{0,8},{8,0},{32,40},{40,32},{64,72},{72,64},{96,104},{104,96},{128... | collective-permute-start | bytes 1548296 | tf_op jit(solution)/shard_map/ppermute | solution.py:32
  41.3 2.3 %collective-permute-start.7 = (bf16[224,1152]{1,0:T(8,128)(2,1)S(1)}, bf16[224,1152]{1,0:T(8,128)(2,1)S(1)}, u32[]{:S(2)}, u32[]{:S(2)}) collective-permute-start(bf16[224,1152]{1,0:T(8,128)(2,1)S(1)} %collective-permute-done.2.fm), channel_id=1, source_target_pairs={{0,8},{8,0},{32,40},{40,32},{64,72},{72,64},{96,104},{104,96},{128... | collective-permute-start | bytes 1548296 | tf_op jit(solution)/shard_map/ppermute | solution.py:32
  41.4 2.9 %collective-permute-start.8 = (bf16[224,1152]{1,0:T(8,128)(2,1)S(1)}, bf16[224,1152]{1,0:T(8,128)(2,1)S(1)}, u32[]{:S(2)}, u32[]{:S(2)}) collective-permute-start(bf16[224,1152]{1,0:T(8,128)(2,1)S(1)} %collective-permute-done.3.em), channel_id=1, source_target_pairs={{0,8},{8,0},{32,40},{40,32},{64,72},{72,64},{96,104},{104,96},{128... | collective-permute-start | bytes 1548296 | tf_op jit(solution)/shard_map/ppermute | solution.py:32
  69.7 9.9 %collective-permute-start.10 = (bf16[288,1152]{1,0:T(8,128)(2,1)S(1)}, bf16[288,1152]{1,0:T(8,128)(2,1)S(1)}, u32[]{:S(2)}, u32[]{:S(2)}) collective-permute-start(bf16[288,1152]{1,0:T(8,128)(2,1)S(1)} %get-tuple-element.48), channel_id=1, source_target_pairs={{0,6},{8,25},{32,38},{40,57},{64,70},{72,89},{96,102},{104,121},{1... | collective-permute-start | bytes 1990664 | tf_op jit(solution)/shard_map/ppermute | solution.py:32
  71.0 11.4 %collective-permute-start.11 = (bf16[288,1152]{1,0:T(8,128)(2,1)S(1)}, bf16[288,1152]{1,0:T(8,128)(2,1)S(1)}, u32[]{:S(2)}, u32[]{:S(2)}) collective-permute-start(bf16[288,1152]{1,0:T(8,128)(2,1)S(1)} %get-tuple-element.49), channel_id=1, source_target_pairs={{0,4},{8,9},{32,36},{40,41},{64,68},{72,73},{96,100},{104,105},{12... | collective-permute-start | bytes 1990664 | tf_op jit(solution)/shard_map/ppermute | solution.py:32
  72.7 16.7 %collective-permute-start.9 = (bf16[288,1152]{1,0:T(8,128)(2,1)S(1)}, bf16[288,1152]{1,0:T(8,128)(2,1)S(1)}, u32[]{:S(2)}, u32[]{:S(2)}) collective-permute-start(bf16[288,1152]{1,0:T(8,128)(2,1)S(1)} %get-tuple-element.47), channel_id=1, source_target_pairs={{0,2},{8,24},{32,34},{40,56},{64,66},{72,88},{96,98},{104,120},{12... | collective-permute-start | bytes 1990664 | tf_op jit(solution)/shard_map/ppermute | solution.py:32
  89.8 5.5 %collective-permute-start.12 = (bf16[72,1152]{1,0:T(8,128)(2,1)S(1)}, bf16[72,1152]{1,0:T(8,128)(2,1)S(1)}, u32[]{:S(2)}, u32[]{:S(2)}) collective-permute-start(bf16[72,1152]{1,0:T(8,128)(2,1)S(1)} %get-tuple-element.50), channel_id=1, source_target_pairs={{0,16},{8,10},{32,48},{40,42},{64,80},{72,74},{96,112},{104,106},{... | collective-permute-start | bytes 497672 | tf_op jit(solution)/shard_map/ppermute | solution.py:32
  90.8 5.8 %collective-permute-start.13 = (bf16[72,1152]{1,0:T(8,128)(2,1)S(1)}, bf16[72,1152]{1,0:T(8,128)(2,1)S(1)}, u32[]{:S(2)}, u32[]{:S(2)}) collective-permute-start(bf16[72,1152]{1,0:T(8,128)(2,1)S(1)} %get-tuple-element.52), channel_id=1, source_target_pairs={{0,17},{8,14},{32,49},{40,46},{64,81},{72,78},{96,113},{104,110},{... | collective-permute-start | bytes 497672 | tf_op jit(solution)/shard_map/ppermute | solution.py:32
  92.6 5.7 %collective-permute-start.14 = (bf16[72,1152]{1,0:T(8,128)(2,1)S(1)}, bf16[72,1152]{1,0:T(8,128)(2,1)S(1)}, u32[]{:S(2)}, u32[]{:S(2)}) collective-permute-start(bf16[72,1152]{1,0:T(8,128)(2,1)S(1)} %get-tuple-element.51), channel_id=1, source_target_pairs={{0,1},{8,12},{32,33},{40,44},{64,65},{72,76},{96,97},{104,108},{12... | collective-permute-start | bytes 497672 | tf_op jit(solution)/shard_map/ppermute | solution.py:32
  112.4 8.9 %collective-permute-start.15 = (f32[81,128]{1,0:T(8,128)S(1)}, f32[81,128]{1,0:T(8,128)S(1)}, u32[]{:S(2)}, u32[]{:S(2)}) collective-permute-start(f32[81,128]{1,0:T(8,128)S(1)} %convert_reduce_fusion), channel_id=1, source_target_pairs={{0,1},{8,0},{32,33},{40,32},{64,65},{72,64},{96,97},{104,96},{128,... | collective-permute-start | bytes 124424 | tf_op jit(solution)/shard_map/ppermute | solution.py:32
  118.1 6.9 %collective-permute-start.16 = (f32[81,128]{1,0:T(8,128)S(1)}, f32[81,128]{1,0:T(8,128)S(1)}, u32[]{:S(2)}, u32[]{:S(2)}) collective-permute-start(f32[81,128]{1,0:T(8,128)S(1)} %convert_reduce_fusion), channel_id=1, source_target_pairs={{8,1},{40,33},{72,65},{104,97},{136,129},{168,161},{200,193},{232,... | collective-permute-start | bytes 124424 | tf_op jit(solution)/shard_map/ppermute | solution.py:32
  125.0 6.2 %copy-start.11 = (f32[2,81,128]{2,1,0:T(8,128)}, f32[2,81,128]{2,1,0:T(8,128)S(1)}, u32[]{:S(2)}) copy-start(f32[2,81,128]{2,1,0:T(8,128)S(1)} %pad_maximum_fusion.one) | copy-start | bytes 248836
  125.0 5.6 %collective-permute-start.17 = (f32[2,81,128]{2,1,0:T(8,128)S(1)}, f32[2,81,128]{2,1,0:T(8,128)S(1)}, u32[]{:S(2)}, u32[]{:S(2)}) collective-permute-start(f32[2,81,128]{2,1,0:T(8,128)S(1)} %pad_maximum_fusion.one), channel_id=1, source_target_pairs={{0,2},{8,10},{32,34},{40,42},{64,66},{72,74},{96,98},{104,106},{12... | collective-permute-start | bytes 248840 | tf_op jit(solution)/shard_map/ppermute | solution.py:32
  125.1 5.5 %collective-permute-start.18 = (f32[2,81,128]{2,1,0:T(8,128)S(1)}, f32[2,81,128]{2,1,0:T(8,128)S(1)}, u32[]{:S(2)}, u32[]{:S(2)}) collective-permute-start(f32[2,81,128]{2,1,0:T(8,128)S(1)} %pad_maximum_fusion.one), channel_id=1, source_target_pairs={{0,4},{8,12},{32,36},{40,44},{64,68},{72,76},{96,100},{104,108},{1... | collective-permute-start | bytes 248840 | tf_op jit(solution)/shard_map/ppermute | solution.py:32
  126.6 4.6 %collective-permute-start.19 = (f32[2,81,128]{2,1,0:T(8,128)S(1)}, f32[2,81,128]{2,1,0:T(8,128)S(1)}, u32[]{:S(2)}, u32[]{:S(2)}) collective-permute-start(f32[2,81,128]{2,1,0:T(8,128)S(1)} %pad_maximum_fusion.one), channel_id=1, source_target_pairs={{0,6},{8,14},{32,38},{40,46},{64,70},{72,78},{96,102},{104,110},{1... | collective-permute-start | bytes 248840 | tf_op jit(solution)/shard_map/ppermute | solution.py:32
  (3 other events, 1.9 us)

commit v3 on v2

--- a/solution.py
+++ b/solution.py
@@ -150,9 +150,9 @@
 
 
 def own_kernel(
-    place_ref, sharp_ref, shift_ref, coef_ref, code_ref, mine_ref, other_ref, im, io, cm, co, wi, wc,
-    pv_out, zx_out, zy_out, ux_out, ix_out, ft_out, dz_out,
-    f, w, pv, tmp, zx, zy, ux, ix, gs, ft, dz, targets, sems,
+    place_ref, sharp_ref, shift_ref, coef_ref, mine_ref, other_ref, im, io, cm, co, wi, wc,
+    zx_out, zy_out, ux_out, ix_out, dz_out,
+    f, w, tmp, zx, zy, ux, ix, gs, dz, targets, sems,
 ):
     core = place_ref[0]
     first = by_role(
@@ -163,8 +163,6 @@
         place_ref, [(cm, io, f.at[1, pl.ds(0, R)]), (co, im, f.at[1, pl.ds(R, R)]), (wc, wi, w.at[1])],
         sems.at[pl.ds(3, 3)],
     )
-    one_hot(place_ref, code_ref, pv)
-    outs = [fetch(pv, pv_out, sems.at[9])]
     targets[...] = jnp.full((2, PAD), -1, jnp.int32)
     targets[0:1, 0:R] = jnp.where(core == 0, mine_ref[...], other_ref[...])
     targets[1:2, 0:R] = jnp.where(core == 0, other_ref[...], mine_ref[...])
@@ -175,7 +173,7 @@
     unit = tmp[...] * inv
     ux[...] = unit
     zx[...] = unit.astype(BF16)
-    outs += [fetch(ux, ux_out, sems.at[6]), fetch(zx, zx_out, sems.at[7]), fetch(ix, ix_out, sems.at[8])]
+    outs = [fetch(ux, ux_out, sems.at[6]), fetch(zx, zx_out, sems.at[7]), fetch(ix, ix_out, sems.at[8])]
     for wait in second:
         wait.wait()
     inv = project(f[1], w.at[1], tmp, 2 * R)
@@ -201,47 +199,76 @@
 
     outs.append(fetch(dz, dz_out, sems.at[11]))
 
-    @pl.loop(0, 3)
-    def _(k):
-        rows = pl.ds(pl.multiple_of(k * 384, 384), 384)
-        ft[rows, 0 : 2 * R] = nt_dot(pv[rows], f[0]).astype(BF16)
-
-    ft[:, 2 * R :] = jnp.zeros((D, 2 * PAD - 2 * R), BF16)
-    for copy in outs + [fetch(ft, ft_out, sems.at[12])]:
+    for copy in outs:
         copy.wait()
 
 
-def own_part(place, sharp, shift, coef, code, mine, other, *operands):
+def own_part(place, sharp, shift, coef, mine, other, *operands):
     smem = pl.BlockSpec(memory_space=pltpu.SMEM)
     vmem = pl.BlockSpec(memory_space=pltpu.VMEM)
     hbm = pl.BlockSpec(memory_space=pl.ANY)
     results = [
-        ((D, D), BF16), ((2 * R, D), BF16), ((2 * PAD, D), BF16), ((2 * R, D), F32), ((2 * R, 128), F32), ((D, 2 * PAD), BF16),
+        ((2 * R, D), BF16), ((2 * PAD, D), BF16), ((2 * R, D), F32), ((2 * R, 128), F32),
         ((2 * R, D), F32),
     ]
     return pl.pallas_call(
         own_kernel,
         out_shape=[jax.ShapeDtypeStruct(*result) for result in results],
-        in_specs=[smem] * 4 + [vmem] * 3 + [hbm] * 6,
-        out_specs=[hbm] * 7,
+        in_specs=[smem] * 4 + [vmem] * 2 + [hbm] * 6,
+        out_specs=[hbm] * 5,
         scratch_shapes=[
             pltpu.VMEM((2, 2 * R, D), BF16),
             pltpu.VMEM((2, D, D), BF16),
-            pltpu.VMEM((D, D), BF16),
             pltpu.VMEM((2 * R, D), F32),
             pltpu.VMEM((2 * R, D), BF16),
             pltpu.VMEM((2 * PAD, D), BF16),
             pltpu.VMEM((2 * R, D), F32),
             pltpu.VMEM((2 * R, 128), F32),
             pltpu.VMEM((2 * R, 2 * PAD), BF16),
-            pltpu.VMEM((D, 2 * PAD), BF16),
             pltpu.VMEM((2 * R, D), F32),
             pltpu.VMEM((2, PAD), jnp.int32),
             pltpu.SemaphoreType.DMA((13,)),
         ],
-        compiler_params=pltpu.CompilerParams(vmem_limit_bytes=30 * 2**20),
+        compiler_params=pltpu.CompilerParams(vmem_limit_bytes=60 * 2**20),
         cost_estimate=pl.CostEstimate(flops=6 * 10**9, bytes_accessed=16 * 10**6, transcendentals=500000),
-    )(place, sharp, shift, coef, code, mine, other, *operands)
+    )(place, sharp, shift, coef, mine, other, *operands)
+
+
+def turn_kernel(place_ref, code_ref, im, io, cm, co, pv_out, ft_out, f, pv, ft, sems):
+    feats = by_role(
+        place_ref, [(im, co, f.at[pl.ds(0, R)]), (io, cm, f.at[pl.ds(R, R)])], sems.at[pl.ds(0, 2)]
+    )
+    one_hot(place_ref, code_ref, pv)
+    outs = [fetch(pv, pv_out, sems.at[2])]
+    for wait in feats:
+        wait.wait()
+
+    @pl.loop(0, 3)
+    def _(k):
+        rows = pl.ds(pl.multiple_of(k * 384, 384), 384)
+        ft[rows, 0 : 2 * R] = nt_dot(pv[rows], f[...]).astype(BF16)
+
+    ft[:, 2 * R :] = jnp.zeros((D, 2 * PAD - 2 * R), BF16)
+    for copy in outs + [fetch(ft, ft_out, sems.at[3])]:
+        copy.wait()
+
+
+def turn_own(place, code, *operands):
+    hbm = pl.BlockSpec(memory_space=pl.ANY)
+    return pl.pallas_call(
+        turn_kernel,
+        out_shape=[jax.ShapeDtypeStruct((D, D), BF16), jax.ShapeDtypeStruct((D, 2 * PAD), BF16)],
+        in_specs=[pl.BlockSpec(memory_space=pltpu.SMEM), pl.BlockSpec(memory_space=pltpu.VMEM)] + [hbm] * 4,
+        out_specs=[hbm] * 2,
+        scratch_shapes=[
+            pltpu.VMEM((2 * R, D), BF16),
+            pltpu.VMEM((D, D), BF16),
+            pltpu.VMEM((D, 2 * PAD), BF16),
+            pltpu.SemaphoreType.DMA((4,)),
+        ],
+        compiler_params=pltpu.CompilerParams(vmem_limit_bytes=60 * 2**20),
+        cost_estimate=pl.CostEstimate(flops=2 * 10**9, bytes_accessed=6 * 10**6, transcendentals=0),
+    )(place, code, *operands)
 
 
 def arrived_kernel(
@@ -403,7 +430,7 @@
             pltpu.VMEM((R, D), F32),
             pltpu.SemaphoreType.DMA((14,)),
         ],
-        compiler_params=pltpu.CompilerParams(vmem_limit_bytes=46 * 2**20),
+        compiler_params=pltpu.CompilerParams(vmem_limit_bytes=60 * 2**20),
         cost_estimate=pl.CostEstimate(flops=14 * 10**9, bytes_accessed=20 * 10**6, transcendentals=800000),
     )(place, sharp, shift, coef, *operands)
 
@@ -458,22 +485,22 @@
     img_far = image_to_neighbour(img)
     img_extra = image_down(img)
 
-    order, *kept = own_part(
-        role, sharpness_param, offset_shift, coefficient, row_code(),
-        matching_target[None], target_other[None],
-        picture_encoder_features, own_img, text_encoder_features, own_cap,
-        picture_projector, text_projector,
-    )
-    cap_sib, img_far, img_extra, order, kept = lax.optimization_barrier(
-        (cap_sib, img_far, img_extra, order, kept)
+    blocks = (picture_encoder_features, own_img, text_encoder_features, own_cap)
+    *kept, from_own = own_part(
+        role, sharpness_param, offset_shift, coefficient, matching_target[None], target_other[None],
+        *blocks, picture_projector, text_projector,
+    )
+    cap_sib, img_far, img_extra, kept, from_own, blocks = lax.optimization_barrier(
+        (cap_sib, img_far, img_extra, kept, from_own, blocks)
     )
     cap_sib_other = swap_cores(cap_sib)
     img_far_other = swap_cores(img_far)
     img_extra_other = swap_cores(img_extra)
+    order, turned = turn_own(role, row_code(), *blocks)
     parts = arrived_part(
         role, sharpness_param, offset_shift, coefficient,
         cap_sib, cap_sib_other, img_far, img_far_other, img_extra, img_extra_other,
-        picture_projector, text_projector, order, *kept,
+        picture_projector, text_projector, order, *kept, turned, from_own,
     )
 
     one = [parts[0]] + [first_axis(parts[by], by) for by in (1, 3, 2)]

time: 134 us -> 126 us (0.940)
  local copies, waits for them, and re-layouts: 13.5 us -> 3.04 us
  Pallas kernels: 41.5 us -> 44.2 us
  other arithmetic: 0.57 us -> 2.19 us
  waiting for transfers between devices: 30.2 us -> 28.6 us
    unnamed x30 -> x26, local copies, waits for them, and re-layouts: 13.3 us -> 2.79 us
    pallas_call x0 -> x1, Pallas kernels: none -> 5.49 us  [turn_own(): pl.pallas_call(turn_kernel, out_shape=[jax.ShapeDtypeStruct((D, D), BF16)...]
    pallas_call x1, Pallas kernels: 14.1 us -> 10.5 us  [own_part(): pl.pallas_call(own_kernel, out_shape=[jax.ShapeDtypeStruct(*result) for r...]
    ppermute x20, waiting for transfers between devices: 30.2 us -> 28.6 us  [moved(): return lax.ppermute(value, AXES, pairs)]
  transfers between devices with their start and end apart: 20 -> 20, of which waited for: 12 -> 10; matrix products, arithmetic and copies ran while one was open for 0% -> 0% of each run, Pallas kernels for 11% -> 13%
where the time goes in v3:
time: 126 us; the launch traced here: 125 us
  Pallas kernels  44.2 us (35%)
  starting transfers between devices  30.7 us (24%)
  waiting for transfers between devices  28.6 us (23%)
  blocking collectives  13.7 us (11%)
  local copies, waits for them, and re-layouts  3.04 us (2%)
  between operations  2.87 us (2%)
  other arithmetic  2.19 us (2%)
    ppermute x20, starting transfers between devices, moved(): return lax.ppermute(value, AXES, pairs)  30.7 us
    ppermute x20, waiting for transfers between devices, moved(): return lax.ppermute(value, AXES, pairs)  28.6 us
    pallas_call x1, Pallas kernels, arrived_part(): pl.pallas_call(arrived_kernel, out_shape=[jax.ShapeDtypeStruct((D // 4, D...  26.1 us
    all_to_all x1, blocking collectives, local(): three = lax.all_to_all(two, AXES, 0, 0, axis_index_groups=ALONG_Z)  13.7 us
    pallas_call x1, Pallas kernels, own_part(): pl.pallas_call(own_kernel, out_shape=[jax.ShapeDtypeStruct(*result) for r...  10.5 us
    pallas_call x1, Pallas kernels, turn_own(): pl.pallas_call(turn_kernel, out_shape=[jax.ShapeDtypeStruct((D, D), BF16)...  5.49 us
    unnamed x26, local copies, waits for them, and re-layouts  2.79 us
  transfers between devices with their start and end apart: 20, of which 10 were waited for; matrix products, arithmetic and copies ran while one was open for 0% of the time, Pallas kernels for 13%

profile of v3, /device:TPU:1, one launch (start us, length us, event | category | flops | bytes accessed | tf_op | source)
XLA Modules:
  0.0 125.3 jit_solution(13156009490530397527)
XLA Ops:
  0.6 3.3 %collective-permute-start.4 = (bf16[224,1152]{1,0:T(8,128)(2,1)}, bf16[224,1152]{1,0:T(8,128)(2,1)S(1)}, u32[]{:S(2)}, u32[]{:S(2)}) collective-permute-start(bf16[224,1152]{1,0:T(8,128)(2,1)} %im.2), channel_id=1, source_target_pairs={{0,8},{8,0},{32,40},{40,32},{64,72},{72,64},{96,104},{104,96},{128... | collective-permute-start | bytes 1548296 | tf_op jit(solution)/shard_map/ppermute | solution.py:32
  7.1 3.9 %collective-permute-start.2 = (bf16[224,1152]{1,0:T(8,128)(2,1)}, bf16[224,1152]{1,0:T(8,128)(2,1)S(1)}, u32[]{:S(2)}, u32[]{:S(2)}) collective-permute-start(bf16[224,1152]{1,0:T(8,128)(2,1)} %im.2), channel_id=1, source_target_pairs={{0,224},{8,232},{32,0},{40,8},{64,32},{72,40},{96,64},{104,72},{12... | collective-permute-start | bytes 1548296 | tf_op jit(solution)/shard_map/ppermute | solution.py:32
  11.0 0.7 collective-permute-start.3
  11.8 0.8 copy-done.4
  12.8 10.5 %shard_map.104 = (bf16[448,1152]{1,0:T(8,128)(2,1)}, bf16[512,1152]{1,0:T(8,128)(2,1)}, f32[448,1152]{1,0:T(8,128)}, f32[448,128]{1,0:T(8,128)}, f32[448,1152]{1,0:T(8,128)}) custom-call(s32[4]{0:T(128)} %pad_add_fusion.place_ref, f32[1]{0:T(128)S(6)} %copy.11.sharp_ref, f32[1]{0:T(128)S(6)} %copy.12.shift_ref, f32[1]{0:T(128)S(6)} %div.24.coef_ref, ...), custom_call_target="tpu_custom_call" | custom-call | flops 6000000000 | bytes 16000000 | tf_op jit(solution)/shard_map/pallas_call | solution.py:214
  23.4 0.7 collective-permute-done.1.sm
  24.1 2.6 %collective-permute-start.6 = (bf16[224,1152]{1,0:T(8,128)(2,1)S(1)}, bf16[224,1152]{1,0:T(8,128)(2,1)S(1)}, u32[]{:S(2)}, u32[]{:S(2)}) collective-permute-start(bf16[224,1152]{1,0:T(8,128)(2,1)S(1)} %collective-permute-done.1.sm), channel_id=1, source_target_pairs={{0,8},{8,0},{32,40},{40,32},{64,72},{72,64},{96,104},{104,96},{128... | collective-permute-start | bytes 1548296 | tf_op jit(solution)/shard_map/ppermute | solution.py:32
  27.1 5.5 %shard_map.105 = (bf16[1152,1152]{1,0:T(8,128)(2,1)}, bf16[1152,512]{1,0:T(8,128)(2,1)}) custom-call(s32[4]{0:T(128)} %pad_add_fusion.place_ref, s32[1152,1]{1,0:T(8,128)} %constant.56.clone.code_ref, bf16[224,1152]{1,0:T(8,128)(2,1)} %im.2, bf16[224,1152]{1,0:T(8,128)(2,1)} %copy-done.4, bf16[224,1152]{1,0:T(8,128)(2,1)} %cm.2, bf16[224,1152]{1,0:T(8,128)(2,1)} %copy-done.5), custom_call_target="tpu_custom_call" | custom-call | flops 2000000000 | bytes 6000000 | tf_op jit(solution)/shard_map/pallas_call | solution.py:258
  32.7 0.7 copy-done.9
  33.8 26.1 %shard_map.106 = (bf16[288,1152]{1,0:T(8,128)(2,1)}, bf16[288,1152]{1,0:T(8,128)(2,1)}, bf16[288,1152]{1,0:T(8,128)(2,1)}, bf16[288,1152]{1,0:T(8,128)(2,1)}) custom-call(s32[4]{0:T(128)} %pad_add_fusion.place_ref, f32[1]{0:T(128)S(6)} %copy.11.sharp_ref, f32[1]{0:T(128)S(6)} %copy.12.shift_ref, f32[1]{0:T(128)S(6)} %div.24.coef_ref, ...), custom_call_target="tpu_custom_call" | custom-call | flops 14000000000 | bytes 20000000 | tf_op jit(solution)/shard_map/pallas_call | solution.py:409
  60.0 1.3 %collective-permute-start.10 = (bf16[288,1152]{1,0:T(8,128)(2,1)}, bf16[288,1152]{1,0:T(8,128)(2,1)S(1)}, u32[]{:S(2)}, u32[]{:S(2)}) collective-permute-start(bf16[288,1152]{1,0:T(8,128)(2,1)} %get-tuple-element.52), channel_id=1, source_target_pairs={{0,6},{8,25},{32,38},{40,57},{64,70},{72,89},{96,102},{104,121},{1... | collective-permute-start | bytes 1990664 | tf_op jit(solution)/shard_map/ppermute | solution.py:32
  61.3 1.5 %collective-permute-start.11 = (bf16[288,1152]{1,0:T(8,128)(2,1)}, bf16[288,1152]{1,0:T(8,128)(2,1)S(1)}, u32[]{:S(2)}, u32[]{:S(2)}) collective-permute-start(bf16[288,1152]{1,0:T(8,128)(2,1)} %get-tuple-element.53), channel_id=1, source_target_pairs={{0,4},{8,9},{32,36},{40,41},{64,68},{72,73},{96,100},{104,105},{12... | collective-permute-start | bytes 1990664 | tf_op jit(solution)/shard_map/ppermute | solution.py:32
  62.8 0.8 collective-permute-start.9
  63.5 6.5 %collective-permute-done.10 = bf16[288,1152]{1,0:T(8,128)(2,1)S(1)} collective-permute-done((bf16[288,1152]{1,0:T(8,128)(2,1)}, bf16[288,1152]{1,0:T(8,128)(2,1)S(1)}, u32[]{:S(2)}, u32[]{:S(2)}) %collective-permute-start.10) | collective-permute-done | bytes 663584 | tf_op jit(solution)/shard_map/ppermute | solution.py:32
  70.1 2.8 %collective-permute-done.11 = bf16[288,1152]{1,0:T(8,128)(2,1)S(1)} collective-permute-done((bf16[288,1152]{1,0:T(8,128)(2,1)}, bf16[288,1152]{1,0:T(8,128)(2,1)S(1)}, u32[]{:S(2)}, u32[]{:S(2)}) %collective-permute-start.11) | collective-permute-done | bytes 663584 | tf_op jit(solution)/shard_map/ppermute | solution.py:32
  72.9 7.1 %collective-permute-done.9 = bf16[288,1152]{1,0:T(8,128)(2,1)S(1)} collective-permute-done((bf16[288,1152]{1,0:T(8,128)(2,1)}, bf16[288,1152]{1,0:T(8,128)(2,1)S(1)}, u32[]{:S(2)}, u32[]{:S(2)}) %collective-permute-start.9) | collective-permute-done | bytes 663584 | tf_op jit(solution)/shard_map/ppermute | solution.py:32
  80.0 1.4 %add_convert_fusion = bf16[288,1152]{1,0:T(8,128)(2,1)S(1)} fusion(bf16[288,1152]{1,0:T(8,128)(2,1)S(1)} %collective-permute-done.11, bf16[288,1152]{1,0:T(8,128)(2,1)S(1)} %collective-permute-done.10, bf16[288,1152]{1,0:T(8,128)(2,1)S(1)} %collective-permute-done.9, bf16[288,1152]{1,0:T(8,128)(2,1)} %get-tuple-element.50), kind=kLoop, calls=%fused_computation | loop fusion | flops 2654208 | bytes 3317760 | tf_op jit(solution)/shard_map/convert_element_type | solution.py:507
  81.4 1.0 collective-permute-start.12
  82.4 1.8 %collective-permute-start.13 = (bf16[72,1152]{1,0:T(8,128)(2,1)S(1)}, bf16[72,1152]{1,0:T(8,128)(2,1)S(1)}, u32[]{:S(2)}, u32[]{:S(2)}) collective-permute-start(bf16[72,1152]{1,0:T(8,128)(2,1)S(1)} %get-tuple-element.56), channel_id=1, source_target_pairs={{0,17},{8,14},{32,49},{40,46},{64,81},{72,78},{96,113},{104,110},{... | collective-permute-start | bytes 497672 | tf_op jit(solution)/shard_map/ppermute | solution.py:32
  84.2 1.3 collective-permute-start.14
  85.4 1.5 %collective-permute-done.12 = bf16[72,1152]{1,0:T(8,128)(2,1)S(1)} collective-permute-done((bf16[72,1152]{1,0:T(8,128)(2,1)S(1)}, bf16[72,1152]{1,0:T(8,128)(2,1)S(1)}, u32[]{:S(2)}, u32[]{:S(2)}) %collective-permute-start.12) | collective-permute-done | bytes 165920 | tf_op jit(solution)/shard_map/ppermute | solution.py:32
  86.9 1.3 %collective-permute-done.13 = bf16[72,1152]{1,0:T(8,128)(2,1)S(1)} collective-permute-done((bf16[72,1152]{1,0:T(8,128)(2,1)S(1)}, bf16[72,1152]{1,0:T(8,128)(2,1)S(1)}, u32[]{:S(2)}, u32[]{:S(2)}) %collective-permute-start.13) | collective-permute-done | bytes 165920 | tf_op jit(solution)/shard_map/ppermute | solution.py:32
  88.3 1.6 %collective-permute-done.14 = bf16[72,1152]{1,0:T(8,128)(2,1)S(1)} collective-permute-done((bf16[72,1152]{1,0:T(8,128)(2,1)S(1)}, bf16[72,1152]{1,0:T(8,128)(2,1)S(1)}, u32[]{:S(2)}, u32[]{:S(2)}) %collective-permute-start.14) | collective-permute-done | bytes 165920 | tf_op jit(solution)/shard_map/ppermute | solution.py:32
  90.2 13.7 %all_to_all.5 = bf16[8,81,128]{2,1,0:T(8,128)(2,1)S(1)} all-to-all(bf16[8,81,128]{2,1,0:T(8,128)(2,1)S(1)} %reshape.7), channel_id=1, replica_groups={{0,32,64,96,128,160,192,224},{8,40,72,104,136,168,200,232},{16,48,80,11..., dimensions={0} | all-to-all | bytes 331776 | tf_op jit(solution)/shard_map/all_to_all | solution.py:511
  104.0 5.5 %collective-permute-start.15 = (f32[81,128]{1,0:T(8,128)S(1)}, f32[81,128]{1,0:T(8,128)S(1)}, u32[]{:S(2)}, u32[]{:S(2)}) collective-permute-start(f32[81,128]{1,0:T(8,128)S(1)} %convert_reduce_fusion), channel_id=1, source_target_pairs={{0,1},{8,0},{32,33},{40,32},{64,65},{72,64},{96,97},{104,96},{128,... | collective-permute-start | bytes 124424 | tf_op jit(solution)/shard_map/ppermute | solution.py:32
  109.5 3.2 %collective-permute-start.16 = (f32[81,128]{1,0:T(8,128)S(1)}, f32[81,128]{1,0:T(8,128)S(1)}, u32[]{:S(2)}, u32[]{:S(2)}) collective-permute-start(f32[81,128]{1,0:T(8,128)S(1)} %convert_reduce_fusion), channel_id=1, source_target_pairs={{8,1},{40,33},{72,65},{104,97},{136,129},{168,161},{200,193},{232,... | collective-permute-start | bytes 124424 | tf_op jit(solution)/shard_map/ppermute | solution.py:32
  112.7 3.6 %collective-permute-done.16 = f32[81,128]{1,0:T(8,128)S(1)} collective-permute-done((f32[81,128]{1,0:T(8,128)S(1)}, f32[81,128]{1,0:T(8,128)S(1)}, u32[]{:S(2)}, u32[]{:S(2)}) %collective-permute-start.16) | collective-permute-done | bytes 41504 | tf_op jit(solution)/shard_map/ppermute | solution.py:32
  116.5 1.5 %collective-permute-start.18 = (f32[2,81,128]{2,1,0:T(8,128)S(1)}, f32[2,81,128]{2,1,0:T(8,128)S(1)}, u32[]{:S(2)}, u32[]{:S(2)}) collective-permute-start(f32[2,81,128]{2,1,0:T(8,128)S(1)} %pad_maximum_fusion.one), channel_id=1, source_target_pairs={{0,4},{8,12},{32,36},{40,44},{64,68},{72,76},{96,100},{104,108},{1... | collective-permute-start | bytes 248840 | tf_op jit(solution)/shard_map/ppermute | solution.py:32
  117.9 1.2 collective-permute-start.19
  119.1 2.9 %collective-permute-done.17.two = f32[2,81,128]{2,1,0:T(8,128)S(1)} collective-permute-done((f32[2,81,128]{2,1,0:T(8,128)S(1)}, f32[2,81,128]{2,1,0:T(8,128)S(1)}, u32[]{:S(2)}, u32[]{:S(2)}) %collective-permute-start.17) | collective-permute-done | bytes 82976 | tf_op jit(solution)/shard_map/ppermute | solution.py:32
  122.7 0.6 copy-done.3
  123.3 2.0 %shard_map.107 = (f32[36,1152]{1,0:T(8,128)}, f32[36,1152]{1,0:T(8,128)}) custom-call(s32[4]{0:T(128)} %pad_add_fusion.place_ref, f32[2,81,128]{2,1,0:T(8,128)} %copy-done, f32[2,81,128]{2,1,0:T(8,128)} %copy-done.1, f32[2,81,128]{2,1,0:T(8,128)} %copy-done.2, f32[2,81,128]{2,1,0:T(8,128)} %copy-done.3), custom_call_target="tpu_custom_call" | custom-call | tf_op jit(solution)/shard_map/pallas_call | solution.py:452
  (47 shorter events, 3.5 us)
Async XLA Ops:
  0.6 11.2 %collective-permute-start.4 = (bf16[224,1152]{1,0:T(8,128)(2,1)}, bf16[224,1152]{1,0:T(8,128)(2,1)S(1)}, u32[]{:S(2)}, u32[]{:S(2)}) collective-permute-start(bf16[224,1152]{1,0:T(8,128)(2,1)} %im.2), channel_id=1, source_target_pairs={{0,8},{8,0},{32,40},{40,32},{64,72},{72,64},{96,104},{104,96},{128... | collective-permute-start | bytes 1548296 | tf_op jit(solution)/shard_map/ppermute | solution.py:32
  4.0 7.8 %collective-permute-start.5 = (bf16[224,1152]{1,0:T(8,128)(2,1)}, bf16[224,1152]{1,0:T(8,128)(2,1)S(1)}, u32[]{:S(2)}, u32[]{:S(2)}) collective-permute-start(bf16[224,1152]{1,0:T(8,128)(2,1)} %cm.2), channel_id=1, source_target_pairs={{0,8},{8,0},{32,40},{40,32},{64,72},{72,64},{96,104},{104,96},{128... | collective-permute-start | bytes 1548296 | tf_op jit(solution)/shard_map/ppermute | solution.py:32
  4.1 3.0 %collective-permute-start = (s32[224]{0:T(256)}, s32[224]{0:T(256)S(1)}, u32[]{:S(2)}, u32[]{:S(2)}) collective-permute-start(s32[224]{0:T(256)} %param.13), channel_id=1, source_target_pairs={{0,8},{8,0},{32,40},{40,32},{64,72},{72,64},{96,104},{104,96},{128... | collective-permute-start | bytes 2696 | tf_op jit(solution)/shard_map/ppermute | solution.py:32
  7.0 4.8 %copy-start.12 = (s32[224]{0:T(256)}, s32[224]{0:T(256)S(1)}, u32[]{:S(2)}) copy-start(s32[224]{0:T(256)S(1)} %collective-permute-done) | copy-start | bytes 2692
  7.1 16.3 %collective-permute-start.2 = (bf16[224,1152]{1,0:T(8,128)(2,1)}, bf16[224,1152]{1,0:T(8,128)(2,1)S(1)}, u32[]{:S(2)}, u32[]{:S(2)}) collective-permute-start(bf16[224,1152]{1,0:T(8,128)(2,1)} %im.2), channel_id=1, source_target_pairs={{0,224},{8,232},{32,0},{40,8},{64,32},{72,40},{96,64},{104,72},{12... | collective-permute-start | bytes 1548296 | tf_op jit(solution)/shard_map/ppermute | solution.py:32
  11.0 12.3 %collective-permute-start.3 = (bf16[224,1152]{1,0:T(8,128)(2,1)}, bf16[224,1152]{1,0:T(8,128)(2,1)S(1)}, u32[]{:S(2)}, u32[]{:S(2)}) collective-permute-start(bf16[224,1152]{1,0:T(8,128)(2,1)} %im.2), channel_id=1, source_target_pairs={{16,240},{48,16},{80,48},{112,80},{144,112},{176,144},{208,176},{2... | collective-permute-start | bytes 1548296 | tf_op jit(solution)/shard_map/ppermute | solution.py:32
  11.7 12.4 %collective-permute-start.1 = (bf16[224,1152]{1,0:T(8,128)(2,1)}, bf16[224,1152]{1,0:T(8,128)(2,1)S(1)}, u32[]{:S(2)}, u32[]{:S(2)}) collective-permute-start(bf16[224,1152]{1,0:T(8,128)(2,1)} %cm.2), channel_id=1, source_target_pairs={{0,16},{8,24},{32,48},{40,56},{64,80},{72,88},{96,112},{104,120},{... | collective-permute-start | bytes 1548296 | tf_op jit(solution)/shard_map/ppermute | solution.py:32
  11.8 0.8 copy-start.4
  11.8 1.0 copy-start.5
  23.3 9.3 %copy-start.6 = (bf16[224,1152]{1,0:T(8,128)(2,1)}, bf16[224,1152]{1,0:T(8,128)(2,1)S(1)}, u32[]{:S(2)}) copy-start(bf16[224,1152]{1,0:T(8,128)(2,1)S(1)} %collective-permute-done.2.fm) | copy-start | bytes 1548292
  23.3 9.3 %copy-start.7 = (bf16[224,1152]{1,0:T(8,128)(2,1)}, bf16[224,1152]{1,0:T(8,128)(2,1)S(1)}, u32[]{:S(2)}) copy-start(bf16[224,1152]{1,0:T(8,128)(2,1)S(1)} %collective-permute-done.3.em) | copy-start | bytes 1548292
  24.1 8.6 %copy-start.8 = (bf16[224,1152]{1,0:T(8,128)(2,1)}, bf16[224,1152]{1,0:T(8,128)(2,1)S(1)}, u32[]{:S(2)}) copy-start(bf16[224,1152]{1,0:T(8,128)(2,1)S(1)} %collective-permute-done.1.sm) | copy-start | bytes 1548292
  24.1 8.6 %collective-permute-start.6 = (bf16[224,1152]{1,0:T(8,128)(2,1)S(1)}, bf16[224,1152]{1,0:T(8,128)(2,1)S(1)}, u32[]{:S(2)}, u32[]{:S(2)}) collective-permute-start(bf16[224,1152]{1,0:T(8,128)(2,1)S(1)} %collective-permute-done.1.sm), channel_id=1, source_target_pairs={{0,8},{8,0},{32,40},{40,32},{64,72},{72,64},{96,104},{104,96},{128... | collective-permute-start | bytes 1548296 | tf_op jit(solution)/shard_map/ppermute | solution.py:32
  26.6 6.1 %collective-permute-start.7 = (bf16[224,1152]{1,0:T(8,128)(2,1)S(1)}, bf16[224,1152]{1,0:T(8,128)(2,1)S(1)}, u32[]{:S(2)}, u32[]{:S(2)}) collective-permute-start(bf16[224,1152]{1,0:T(8,128)(2,1)S(1)} %collective-permute-done.2.fm), channel_id=1, source_target_pairs={{0,8},{8,0},{32,40},{40,32},{64,72},{72,64},{96,104},{104,96},{128... | collective-permute-start | bytes 1548296 | tf_op jit(solution)/shard_map/ppermute | solution.py:32
  26.7 6.0 %collective-permute-start.8 = (bf16[224,1152]{1,0:T(8,128)(2,1)S(1)}, bf16[224,1152]{1,0:T(8,128)(2,1)S(1)}, u32[]{:S(2)}, u32[]{:S(2)}) collective-permute-start(bf16[224,1152]{1,0:T(8,128)(2,1)S(1)} %collective-permute-done.3.em), channel_id=1, source_target_pairs={{0,8},{8,0},{32,40},{40,32},{64,72},{72,64},{96,104},{104,96},{128... | collective-permute-start | bytes 1548296 | tf_op jit(solution)/shard_map/ppermute | solution.py:32
  32.7 0.8 copy-start.9
  32.7 1.0 copy-start.10
  32.7 1.1 copy-start.11
  60.0 10.1 %collective-permute-start.10 = (bf16[288,1152]{1,0:T(8,128)(2,1)}, bf16[288,1152]{1,0:T(8,128)(2,1)S(1)}, u32[]{:S(2)}, u32[]{:S(2)}) collective-permute-start(bf16[288,1152]{1,0:T(8,128)(2,1)} %get-tuple-element.52), channel_id=1, source_target_pairs={{0,6},{8,25},{32,38},{40,57},{64,70},{72,89},{96,102},{104,121},{1... | collective-permute-start | bytes 1990664 | tf_op jit(solution)/shard_map/ppermute | solution.py:32
  61.3 11.6 %collective-permute-start.11 = (bf16[288,1152]{1,0:T(8,128)(2,1)}, bf16[288,1152]{1,0:T(8,128)(2,1)S(1)}, u32[]{:S(2)}, u32[]{:S(2)}) collective-permute-start(bf16[288,1152]{1,0:T(8,128)(2,1)} %get-tuple-element.53), channel_id=1, source_target_pairs={{0,4},{8,9},{32,36},{40,41},{64,68},{72,73},{96,100},{104,105},{12... | collective-permute-start | bytes 1990664 | tf_op jit(solution)/shard_map/ppermute | solution.py:32
  62.8 17.2 %collective-permute-start.9 = (bf16[288,1152]{1,0:T(8,128)(2,1)}, bf16[288,1152]{1,0:T(8,128)(2,1)S(1)}, u32[]{:S(2)}, u32[]{:S(2)}) collective-permute-start(bf16[288,1152]{1,0:T(8,128)(2,1)} %get-tuple-element.51), channel_id=1, source_target_pairs={{0,2},{8,24},{32,34},{40,56},{64,66},{72,88},{96,98},{104,120},{12... | collective-permute-start | bytes 1990664 | tf_op jit(solution)/shard_map/ppermute | solution.py:32
  81.4 5.5 %collective-permute-start.12 = (bf16[72,1152]{1,0:T(8,128)(2,1)S(1)}, bf16[72,1152]{1,0:T(8,128)(2,1)S(1)}, u32[]{:S(2)}, u32[]{:S(2)}) collective-permute-start(bf16[72,1152]{1,0:T(8,128)(2,1)S(1)} %get-tuple-element.54), channel_id=1, source_target_pairs={{0,16},{8,10},{32,48},{40,42},{64,80},{72,74},{96,112},{104,106},{... | collective-permute-start | bytes 497672 | tf_op jit(solution)/shard_map/ppermute | solution.py:32
  82.4 5.8 %collective-permute-start.13 = (bf16[72,1152]{1,0:T(8,128)(2,1)S(1)}, bf16[72,1152]{1,0:T(8,128)(2,1)S(1)}, u32[]{:S(2)}, u32[]{:S(2)}) collective-permute-start(bf16[72,1152]{1,0:T(8,128)(2,1)S(1)} %get-tuple-element.56), channel_id=1, source_target_pairs={{0,17},{8,14},{32,49},{40,46},{64,81},{72,78},{96,113},{104,110},{... | collective-permute-start | bytes 497672 | tf_op jit(solution)/shard_map/ppermute | solution.py:32
  84.2 5.7 %collective-permute-start.14 = (bf16[72,1152]{1,0:T(8,128)(2,1)S(1)}, bf16[72,1152]{1,0:T(8,128)(2,1)S(1)}, u32[]{:S(2)}, u32[]{:S(2)}) collective-permute-start(bf16[72,1152]{1,0:T(8,128)(2,1)S(1)} %get-tuple-element.55), channel_id=1, source_target_pairs={{0,1},{8,12},{32,33},{40,44},{64,65},{72,76},{96,97},{104,108},{12... | collective-permute-start | bytes 497672 | tf_op jit(solution)/shard_map/ppermute | solution.py:32
  104.0 8.7 %collective-permute-start.15 = (f32[81,128]{1,0:T(8,128)S(1)}, f32[81,128]{1,0:T(8,128)S(1)}, u32[]{:S(2)}, u32[]{:S(2)}) collective-permute-start(f32[81,128]{1,0:T(8,128)S(1)} %convert_reduce_fusion), channel_id=1, source_target_pairs={{0,1},{8,0},{32,33},{40,32},{64,65},{72,64},{96,97},{104,96},{128,... | collective-permute-start | bytes 124424 | tf_op jit(solution)/shard_map/ppermute | solution.py:32
  109.5 6.9 %collective-permute-start.16 = (f32[81,128]{1,0:T(8,128)S(1)}, f32[81,128]{1,0:T(8,128)S(1)}, u32[]{:S(2)}, u32[]{:S(2)}) collective-permute-start(f32[81,128]{1,0:T(8,128)S(1)} %convert_reduce_fusion), channel_id=1, source_target_pairs={{8,1},{40,33},{72,65},{104,97},{136,129},{168,161},{200,193},{232,... | collective-permute-start | bytes 124424 | tf_op jit(solution)/shard_map/ppermute | solution.py:32
  116.3 6.2 %copy-start = (f32[2,81,128]{2,1,0:T(8,128)}, f32[2,81,128]{2,1,0:T(8,128)S(1)}, u32[]{:S(2)}) copy-start(f32[2,81,128]{2,1,0:T(8,128)S(1)} %pad_maximum_fusion.one) | copy-start | bytes 248836
  116.4 5.6 %collective-permute-start.17 = (f32[2,81,128]{2,1,0:T(8,128)S(1)}, f32[2,81,128]{2,1,0:T(8,128)S(1)}, u32[]{:S(2)}, u32[]{:S(2)}) collective-permute-start(f32[2,81,128]{2,1,0:T(8,128)S(1)} %pad_maximum_fusion.one), channel_id=1, source_target_pairs={{0,2},{8,10},{32,34},{40,42},{64,66},{72,74},{96,98},{104,106},{12... | collective-permute-start | bytes 248840 | tf_op jit(solution)/shard_map/ppermute | solution.py:32
  116.5 5.5 %collective-permute-start.18 = (f32[2,81,128]{2,1,0:T(8,128)S(1)}, f32[2,81,128]{2,1,0:T(8,128)S(1)}, u32[]{:S(2)}, u32[]{:S(2)}) collective-permute-start(f32[2,81,128]{2,1,0:T(8,128)S(1)} %pad_maximum_fusion.one), channel_id=1, source_target_pairs={{0,4},{8,12},{32,36},{40,44},{64,68},{72,76},{96,100},{104,108},{1... | collective-permute-start | bytes 248840 | tf_op jit(solution)/shard_map/ppermute | solution.py:32
  117.9 4.6 %collective-permute-start.19 = (f32[2,81,128]{2,1,0:T(8,128)S(1)}, f32[2,81,128]{2,1,0:T(8,128)S(1)}, u32[]{:S(2)}, u32[]{:S(2)}) collective-permute-start(f32[2,81,128]{2,1,0:T(8,128)S(1)} %pad_maximum_fusion.one), channel_id=1, source_target_pairs={{0,6},{8,14},{32,38},{40,46},{64,70},{72,78},{96,102},{104,110},{1... | collective-permute-start | bytes 248840 | tf_op jit(solution)/shard_map/ppermute | solution.py:32
  122.0 0.6 copy-start.1
  122.0 0.7 copy-start.2
  (1 other events, 0.6 us)
